TPU v7x, 128 devices: a whole 4x4x4 slice. The times are simulated.
128 devices in a mesh: dp: 32 (over z, y, x_hi), mp: 4 (over x_lo, core).
Axes of the slice: x: 4 (x_hi: 2, x_lo: 2; x = x_hi * 2 + x_lo), y: 4, z: 4, core: 2. Of those that a mesh axis runs over, the one named last changes fastest.
Arguments:
- tokens: bfloat16 [16384, 8192], P(('dp', 'mp')), may hold values from -24 to 24
- gain: float32 [8192], replicated, may hold values from 0.1 to 1.9
- query: bfloat16 [16384, 8192], P('dp', 'mp'), may hold values from -64 to 64
- query_tangent: bfloat16 [16384, 8192], P('dp', 'mp'), may hold values from -6 to 6
- kv_weight: bfloat16 [2, 8192, 1024], P(None, 'dp', 'mp'), may hold values from -0.0625 to 0.0625
- kv_bias: float32 [2, 1024], P(None, 'mp'), may hold values from -3 to 3
- kv_task: bfloat16 [2, 8192, 1024], P(None, 'dp', 'mp'), may hold values from -0.0625 to 0.0625
- kv_bias_task: float32 [2, 1024], P(None, 'mp'), may hold values from -3 to 3
- cotangent: bfloat16 [16384, 8192], P('dp', 'mp'), may hold values from -0.046875 to 0.046875
Outputs:
- context: bfloat16 [16384, 8192], P('dp', 'mp')
- context_tangent: bfloat16 [16384, 8192], P('dp', 'mp')
- kv_grad: float32 [2, 8192, 1024], P(None, 'dp', 'mp')
- kv_bias_grad: float32 [2, 1024], P(None, 'mp')
All inputs are finite; a program needn't handle non-finite values.
Results may differ from a plain program's by a relative error of at most 0.03.
The roundings to bfloat16 on the way count: a program that leaves them out, or rounds other values in their place, can miss the bound.
Values may be sent and summed in bfloat16 or wider, within the bound.
A program may use at most 192 MiB of HBM per device.

v0:
```python
import jax
import jax.numpy as jnp
from jax import lax
from jax.sharding import PartitionSpec as P

HEAD = 128


def rotate(field, sign):
    length = field.shape[0]
    width = field.shape[-1]
    half_width = width // 2
    position = jnp.arange(length).astype(jnp.float32)
    frequency = jnp.power(1000000.0, -2.0 * jnp.arange(half_width).astype(jnp.float32) / width)
    angle = position[:, None] * frequency[None, :]
    angle = jnp.concatenate([angle, angle], axis=-1)
    cosine = jnp.cos(angle)[:, None, :]
    sine = sign * jnp.sin(angle)[:, None, :]
    turned = jnp.concatenate([-field[..., half_width:], field[..., :half_width]], axis=-1)
    return field * cosine + turned * sine


def multiply(form, left, right):
    return jnp.einsum(form, left, right, preferred_element_type=jnp.float32)


def attend(queries, query_tangent, cotangent, keys, values, key_tangent, value_tangent):
    factor = HEAD ** (-0.5)
    length = queries.shape[0]
    causal = jnp.arange(length)[:, None] >= jnp.arange(length)[None, :]
    scores = multiply("tkgh,skh->kgts", queries, keys) * factor
    scores = jnp.where(causal, scores, -jnp.inf)
    highest = jnp.max(scores, axis=-1, keepdims=True)
    raised = jnp.exp(scores - highest)
    weights = raised / jnp.sum(raised, axis=-1, keepdims=True)
    weights16 = weights.astype(jnp.bfloat16)
    context = multiply("kgts,skh->tkgh", weights16, values)
    spread = (
        multiply("tkgh,skh->kgts", query_tangent, keys)
        + multiply("tkgh,skh->kgts", queries, key_tangent)
    ) * factor
    moved = weights * (spread - jnp.sum(weights * spread, axis=-1, keepdims=True))
    moved16 = moved.astype(jnp.bfloat16)
    context_tangent = multiply("kgts,skh->tkgh", moved16, values) + multiply(
        "kgts,skh->tkgh", weights16, value_tangent
    )
    value_back = multiply("kgts,tkgh->skh", weights16, cotangent)
    pulled = multiply("tkgh,skh->kgts", cotangent, values)
    score_back = (
        weights * (pulled - jnp.sum(weights * pulled, axis=-1, keepdims=True)) * factor
    ).astype(jnp.bfloat16)
    key_turned = multiply("kgts,tkgh->skh", score_back, queries)
    return (context, context_tangent, key_turned, value_back)


def body(tokens, gain, query, query_tangent, kv_weight, kv_bias, kv_task, kv_bias_task, cotangent):
    wide = tokens.astype(jnp.float32)
    normed = (
        wide * lax.rsqrt(jnp.mean(wide * wide, axis=-1, keepdims=True) + 1e-06) * gain
    ).astype(jnp.bfloat16)
    normed_all = lax.all_gather(normed, "mp", axis=0, tiled=True)
    length = normed_all.shape[0]
    local_width = kv_weight.shape[2]
    local_heads = local_width // HEAD

    def add_rows(weight_rows):
        return multiply("td,kdc->ktc", normed_all, weight_rows)

    base_kv = add_rows(lax.all_gather(kv_weight, "dp", axis=1, tiled=True))
    task_kv = add_rows(lax.all_gather(kv_task, "dp", axis=1, tiled=True))
    base_kv = base_kv + kv_bias[:, None, :]
    task_kv = task_kv + kv_bias_task[:, None, :]
    heads_shape = (length, local_heads, HEAD)
    keys = rotate(base_kv[0].reshape(heads_shape), 1.0).astype(jnp.bfloat16)
    values = base_kv[1].reshape(heads_shape).astype(jnp.bfloat16)
    key_tangent = rotate(task_kv[0].reshape(heads_shape), 1.0).astype(jnp.bfloat16)
    value_tangent = task_kv[1].reshape(heads_shape).astype(jnp.bfloat16)
    grouped = (length, local_heads, -1, HEAD)
    queries = query.reshape(grouped)
    tangents = query_tangent.reshape(grouped)
    cotangents = cotangent.reshape(grouped)
    results = []
    for head_index in range(local_heads):
        pick = slice(head_index, head_index + 1)
        results.append(
            attend(
                queries[:, pick],
                tangents[:, pick],
                cotangents[:, pick],
                keys[:, pick],
                values[:, pick],
                key_tangent[:, pick],
                value_tangent[:, pick],
            )
        )
    context = (
        jnp.concatenate([item[0] for item in results], axis=1)
        .reshape(length, -1)
        .astype(jnp.bfloat16)
    )
    context_tangent = (
        jnp.concatenate([item[1] for item in results], axis=1)
        .reshape(length, -1)
        .astype(jnp.bfloat16)
    )
    key_turned = jnp.concatenate([item[2] for item in results], axis=1)
    value_back = jnp.concatenate([item[3] for item in results], axis=1).reshape(length, local_width)
    key_back = rotate(key_turned, -1.0).reshape(length, local_width)
    back16 = jnp.stack([key_back, value_back]).astype(jnp.bfloat16)
    scattered = lax.psum_scatter(
        multiply("td,ktc->dkc", normed_all, back16).astype(jnp.bfloat16),
        "dp",
        scatter_dimension=0,
        tiled=True,
    ).astype(jnp.float32)
    kv_grad = jnp.transpose(scattered, (1, 0, 2))
    unit_column = jnp.ones((length,), jnp.bfloat16)
    kv_bias_grad = lax.psum(multiply("t,ktc->kc", unit_column, back16), "dp")
    return (context, context_tangent, kv_grad, kv_bias_grad)


def solution(mesh):
    in_specs = (
        P(("dp", "mp"), None),
        P(),
        P("dp", "mp"),
        P("dp", "mp"),
        P(None, "dp", "mp"),
        P(None, "mp"),
        P(None, "dp", "mp"),
        P(None, "mp"),
        P("dp", "mp"),
    )
    out_specs = (P("dp", "mp"), P("dp", "mp"), P(None, "dp", "mp"), P(None, "mp"))
    return jax.shard_map(body, mesh=mesh, in_specs=in_specs, out_specs=out_specs, check_vma=False)
```

profile of v0, /device:TPU:0, one launch (start us, length us, event | category | flops | bytes accessed | tf_op | source)
XLA Modules:
  0.0 620.3 jit_solution(5228889166365027388)
XLA Ops:
  7.2 2.2 fusion.25
  9.5 3.5 fusion.27
  14.9 2.5 copy.49
  17.4 2.9 copy.44
  20.3 4.0 copy.60
  24.5 1.9 broadcast_multiply_fusion
  26.4 69.4 %all-gather.4.cloned.1.call-done = bf16[512,8192]{1,0:T(8,128)(2,1)} async-done(((bf16[128,8192]{1,0:T(8,128)(2,1)}), bf16[512,8192]{1,0:T(8,128)(2,1)}) %all-gather.4.cloned.1.call-update) | async-done | bytes 8388624 | tf_op jit(solution)/shard_map/all_gather | solution.py:61
  95.8 105.8 %all-gather.6.cloned.1.call-done = bf16[2,8192,256]{1,2,0:T(8,128)(2,1)} async-done(((bf16[2,256,256]{1,2,0:T(8,128)(2,1)}), bf16[2,8192,256]{1,2,0:T(8,128)(2,1)}) %all-gather.6.cloned.1.call-update) | async-done | bytes 8388624 | tf_op jit(solution)/shard_map/all_gather | solution.py:69
  201.5 9.4 %fusion.79 = f32[2,512,256]{1,2,0:T(8,128)S(1)} fusion(bf16[2,8192,256]{1,2,0:T(8,128)(2,1)} %all-gather.6.cloned.1.call-done, bf16[512,8192]{1,0:T(8,128)(2,1)} %all-gather.4.cloned.1.call-done, f32[2,256]{1,0:T(2,128)S(1)} %copy-done.19), kind=kOutput, calls=%fused_computation.78 | convolution fusion | flops 4295229440 | bytes 17827840 | tf_op jit(solution)/shard_map/td,kdc->ktc/dot_general | solution.py:24
  212.1 91.7 %all-gather.8.cloned.1.call-done = bf16[2,8192,256]{1,2,0:T(8,128)(2,1)} async-done(((bf16[2,256,256]{1,2,0:T(8,128)(2,1)}), bf16[2,8192,256]{1,2,0:T(8,128)(2,1)}) %all-gather.8.cloned.1.call-update) | async-done | bytes 8388624 | tf_op jit(solution)/shard_map/all_gather | solution.py:70
  303.9 9.9 %fusion.85 = f32[2,512,256]{1,2,0:T(8,128)S(1)} fusion(bf16[2,8192,256]{1,2,0:T(8,128)(2,1)} %all-gather.8.cloned.1.call-done, bf16[512,8192]{1,0:T(8,128)(2,1)} %all-gather.4.cloned.1.call-done, f32[2,256]{1,0:T(2,128)S(1)} %copy-done.20), kind=kOutput, calls=%fused_computation.80 | convolution fusion | flops 4295229440 | bytes 17827840 | tf_op jit(solution)/shard_map/td,kdc->ktc/dot_general | solution.py:24
  321.8 4.5 add_multiply_fusion
  326.3 4.5 add_multiply_fusion.1
  332.3 3.3 fusion.20
  338.8 4.7 fusion.115
  343.5 2.6 fusion.109
  346.1 3.2 fusion.106
  349.3 20.9 %fusion.4 = (f32[8,512]{1,0:T(8,128)S(1)}, f32[8,512]{1,0:T(8,128)}, f32[8,512]{1,0:T(8,128)}, f32[8,512]{1,0:T(8,128)S(1)}, f32[512,512,8]{1,0,2:T(8,128)}) fusion(f32[8,512]{1,0:T(8,128)S(1)} %get-tuple-element.18, f32[8,512]{1,0:T(8,128)S(1)} %get-tuple-element.31, f32[512,512,8]{1,0,2:T(8,128)} %copy-done.1, pred[512,512]{0,1:T(8,128)(4,1)S(1)} %iota_compare_fusion, ...), kind=kOutput, calls=%fused_computation.11 | convolution fusion | flops 570408960 | bytes 51904512 | tf_op jit(solution)/shard_map/tkgh,skh->kgts/dot_general | solution.py:24
  370.3 7.8 %fusion.97 = f32[512,1,128]{2,0,1:T(8,128)S(1)} fusion(f32[512,512,8]{1,0,2:T(8,128)} %fusion.115, f32[8,512]{1,0:T(8,128)S(1)} %get-tuple-element.17, bf16[512,2,8,128]{0,3,2,1:T(8,128)(2,1)S(1)} %bitcast.368, f32[512,512,8]{1,0,2:T(8,128)} %copy-done.3, f32[8,512]{1,0:T(8,128)S(1)} %fusion.22, f32[8,512]{1,0:T(8,128)S(1)} %get-tuple-element.19, ...), kind=kOutput, calls=%fused_computation.84 | convolution fusion | flops 553648128 | bytes 18399232 | tf_op jit(solution)/shard_map/kgts,tkgh->skh/dot_general | solution.py:24
  378.5 2.4 copy-done.21
  380.9 3.1 fusion.94
  385.9 10.3 %convolution_convert_fusion = bf16[8192,2,256]{2,0,1:T(8,128)(2,1)} fusion(bf16[512,8192]{1,0:T(8,128)(2,1)} %all-gather.4.cloned.1.call-done, bf16[1,512,256]{2,1,0:T(8,128)(2,1)S(1)} %copy.77, bf16[1,512,256]{2,1,0:T(8,128)(2,1)S(1)} %copy.76), kind=kOutput, calls=%fused_computation | convolution fusion | flops 4300210176 | bytes 17301504 | tf_op jit(solution)/shard_map/td,ktc->dkc/dot_general | solution.py:24
  397.5 7.5 %fusion.29 = f32[128,8,512]{2,0,1:T(8,128)S(1)} fusion(f32[512,512,8]{1,0,2:T(8,128)} %add_multiply_fusion.1, f32[8,512]{1,0:T(8,128)S(1)} %copy-done.25, bf16[512,2,128]{0,2,1:T(8,128)(2,1)S(1)} %bitcast.387, f32[512,512,8]{1,0,2:T(8,128)} %copy-done.1, f32[8,512]{1,0:T(8,128)S(1)} %copy-done.23, f32[8,512]{1,0:T(8,128)S(1)} %copy-done.16, ...), kind=kOutput, calls=%fused_computation.46 | convolution fusion | flops 551550976 | bytes 19316736 | tf_op jit(solution)/shard_map/kgts,skh->tkgh/dot_general | solution.py:24
  405.0 6.2 %fusion.70 = bf16[512,1,8,128]{0,3,2,1:T(8,128)(2,1)S(1)} fusion(f32[128,8,512]{2,0,1:T(8,128)S(1)} %fusion.29, bf16[512,2,128]{0,2,1:T(8,128)(2,1)S(1)} %bitcast.390, f32[512,512,8]{1,0,2:T(8,128)} %copy-done.1, f32[8,512]{1,0:T(8,128)S(1)} %copy-done.23, f32[8,512]{1,0:T(8,128)S(1)} %copy-done.16, pred[512,512]{0,1:T(8,128)(4,1)S(1)} %iota_compare_fusion), kind=kOutput, calls=%fused_computation.75 | convolution fusion | flops 548405248 | bytes 11960320 | tf_op jit(solution)/shard_map/kgts,skh->tkgh/dot_general | solution.py:24
  411.3 7.6 %fusion.32 = f32[128,8,512]{2,0,1:T(8,128)S(1)} fusion(f32[512,512,8]{1,0,2:T(8,128)} %add_multiply_fusion, f32[8,512]{1,0:T(8,128)S(1)} %copy-done.24, bf16[512,2,128]{0,2,1:T(8,128)(2,1)S(1)} %bitcast.388, f32[512,512,8]{1,0,2:T(8,128)} %copy-done.3, f32[8,512]{1,0:T(8,128)S(1)} %copy-done.18, f32[8,512]{1,0:T(8,128)S(1)} %get-tuple-element.19, ...), kind=kOutput, calls=%fused_computation.48 | convolution fusion | flops 551550976 | bytes 19316736 | tf_op jit(solution)/shard_map/kgts,skh->tkgh/dot_general | solution.py:24
  419.0 3.0 fusion.73
  422.1 2.4 copy.80
  424.5 6.1 fusion.67
  430.7 6.0 fusion.64
  436.9 2.4 copy.79
  439.3 95.7 %psum.7 = f32[2,256]{1,0:T(2,128)} all-reduce(f32[2,256]{1,0:T(2,128)S(1)} %bitcast.392), channel_id=1, replica_groups=mesh['dp'=32,'mp'=4] {'dp'}, use_global_device_ids=true, to_apply=%region_10.11 | all-reduce | flops 512 | bytes 4096 | tf_op jit(solution)/shard_map/psum | solution.py:118
  535.0 76.6 %reduce-scatter.2.cloned.1.call-done = bf16[256,2,256]{2,0,1:T(8,128)(2,1)} async-done(((bf16[8192,2,256]{2,0,1:T(8,128)(2,1)}), bf16[256,2,256]{2,0,1:T(8,128)(2,1)}) %reduce-scatter.2.cloned.1.call-update) | async-done | bytes 262160 | tf_op jit(solution)/shard_map/reduce_scatter | solution.py:110
  (94 shorter events, 21.6 us)
Async XLA Ops:
  7.2 5.9 copy-start.13
  7.2 6.8 %copy-start.14 = (bf16[2,256,256]{2,1,0:T(8,128)(2,1)S(1)}, bf16[2,256,256]{2,1,0:T(8,128)(2,1)}, u32[]{:S(2)}) copy-start(bf16[2,256,256]{2,1,0:T(8,128)(2,1)} %param.15) | copy-start | bytes 786436
  7.2 7.7 %copy-start.6 = (bf16[512,2048]{1,0:T(8,128)(2,1)S(1)}, bf16[512,2048]{1,0:T(8,128)(2,1)}, u32[]{:S(2)}) copy-start(bf16[512,2048]{1,0:T(8,128)(2,1)} %param.12) | copy-start | bytes 6291460
  7.2 88.6 %all-gather.4.cloned.1.call-start = ((), (), s32[]{:S(2)}) async-start(), calls=%async_computation.1 | async-start | bytes 10485760 | tf_op jit(solution)/shard_map/all_gather | solution.py:61
  13.0 188.5 %copy-start.19 = (f32[2,256]{1,0:T(2,128)S(1)}, f32[2,256]{1,0:T(2,128)}, u32[]{:S(2)}) copy-start(f32[2,256]{1,0:T(2,128)} %param.14) | copy-start | bytes 6148
  13.0 188.5 %all-gather.6.cloned.1.call-start = ((), (), s32[]{:S(2)}) async-start(), calls=%async_computation.2 | async-start | bytes 8650752 | tf_op jit(solution)/shard_map/all_gather | solution.py:69
  13.9 289.9 %all-gather.8.cloned.1.call-start = ((), (), s32[]{:S(2)}) async-start(), calls=%async_computation.3 | async-start | bytes 8650752 | tf_op jit(solution)/shard_map/all_gather | solution.py:70
  14.9 596.7 %reduce-scatter.2.cloned.1.call-start = ((), (), s32[]{:S(2)}) async-start(), calls=%async_computation.4 | async-start | bytes 8650752 | tf_op jit(solution)/shard_map/reduce_scatter | solution.py:110
  26.4 277.5 %copy-start.20 = (f32[2,256]{1,0:T(2,128)S(1)}, f32[2,256]{1,0:T(2,128)}, u32[]{:S(2)}) copy-start(f32[2,256]{1,0:T(2,128)} %param.16) | copy-start | bytes 6148
  211.0 1.0 copy-start.12
  313.8 1.2 copy-start.11
  316.2 2.0 copy-start
  321.8 27.6 %copy-start.8 = (bf16[1,512,256]{1,2,0:T(8,128)(2,1)}, bf16[1,512,256]{1,2,0:T(8,128)(2,1)S(1)}, u32[]{:S(2)}) copy-start(bf16[1,512,256]{1,2,0:T(8,128)(2,1)S(1)} %slice.183) | copy-start | bytes 786436
  332.2 13.8 %copy-start.1 = (f32[512,512,8]{1,0,2:T(8,128)}, f32[512,512,8]{1,0,2:T(8,128)S(1)}, u32[]{:S(2)}) copy-start(f32[512,512,8]{1,0,2:T(8,128)S(1)} %get-tuple-element.32) | copy-start | bytes 25165828
  332.3 45.8 %copy-start.15 = (f32[8,512]{1,0:T(8,128)}, f32[8,512]{1,0:T(8,128)S(1)}, u32[]{:S(2)}) copy-start(f32[8,512]{1,0:T(8,128)S(1)} %get-tuple-element.31) | copy-start | bytes 49156
  335.6 7.9 %copy-start.3 = (f32[512,512,8]{1,0,2:T(8,128)}, f32[512,512,8]{1,0,2:T(8,128)S(1)}, u32[]{:S(2)}) copy-start(f32[512,512,8]{1,0,2:T(8,128)S(1)} %get-tuple-element.33) | copy-start | bytes 25165828
  335.6 42.4 %copy-start.22 = (f32[8,512]{1,0:T(8,128)}, f32[8,512]{1,0:T(8,128)S(1)}, u32[]{:S(2)}) copy-start(f32[8,512]{1,0:T(8,128)S(1)} %get-tuple-element.18) | copy-start | bytes 49156
  335.6 3.2 copy-start.4
  337.4 32.9 %copy-start.17 = (f32[8,512]{1,0:T(8,128)}, f32[8,512]{1,0:T(8,128)S(1)}, u32[]{:S(2)}) copy-start(f32[8,512]{1,0:T(8,128)S(1)} %fusion.22) | copy-start | bytes 49156
  370.3 8.2 %copy-start.2 = (f32[512,512,8]{1,0,2:T(8,128)S(1)}, f32[512,512,8]{1,0,2:T(8,128)}, u32[]{:S(2)}) copy-start(f32[512,512,8]{1,0,2:T(8,128)} %copy-done.1) | copy-start | bytes 25165828
  370.3 10.6 %copy-start.21 = (f32[512,512,8]{1,0,2:T(8,128)S(1)}, f32[512,512,8]{1,0,2:T(8,128)}, u32[]{:S(2)}) copy-start(f32[512,512,8]{1,0,2:T(8,128)} %get-tuple-element.34) | copy-start | bytes 25165828
  380.9 3.4 copy-start.5
  380.9 3.4 copy-start.7
  396.2 1.3 copy-start.9
  396.2 1.3 copy-start.16
  396.2 1.3 copy-start.23
  396.2 1.3 copy-start.25
  405.0 6.3 %copy-start.18 = (f32[8,512]{1,0:T(8,128)S(1)}, f32[8,512]{1,0:T(8,128)}, u32[]{:S(2)}) copy-start(f32[8,512]{1,0:T(8,128)} %copy-done.17) | copy-start | bytes 49156
  405.0 6.3 %copy-start.24 = (f32[8,512]{1,0:T(8,128)S(1)}, f32[8,512]{1,0:T(8,128)}, u32[]{:S(2)}) copy-start(f32[8,512]{1,0:T(8,128)} %get-tuple-element.16) | copy-start | bytes 49156
  405.0 13.9 %slice-start = ((s8[8388608]{0:T(1024)(128)(4,1)}), s8[4194304]{0:T(1024)(128)(4,1)S(1)}, s32[]{:S(2)}) async-start(s8[8388608]{0:T(1024)(128)(4,1)} %bitcast.372), calls=%async_computation.5 | async-start | bytes 8388608
  411.3 7.7 %slice-start.1 = ((s8[8388608]{0:T(1024)(128)(4,1)}), s8[4194304]{0:T(1024)(128)(4,1)S(1)}, s32[]{:S(2)}) async-start(s8[8388608]{0:T(1024)(128)(4,1)} %bitcast.372), calls=%async_computation.6 | async-start | bytes 8388608
  424.5 6.1 copy-start.10
Sparse Core Ops, SparseCore 0:
  13.1 82.5 all-gather.3
  99.1 102.3 all-gather.5
  204.3 99.5 all-gather.7
  396.3 215.2 reduce-scatter.1
where the time goes:
time: 627 us; the launch traced here: 620 us
  waiting for transfers between devices  344 us (55%)
  matrix products  125 us (20%)
  blocking collectives  95.7 us (15%)
  local copies, waits for them, and re-layouts  26.3 us (4%)
  other arithmetic  15.1 us (2%)
  between operations  14.7 us (2%)
    dot_general x22, matrix products, multiply(): return jnp.einsum(form, left, right, preferred_element_type=jnp.float32)  125 us
    all_gather x1, waiting for transfers between devices, body(): base_kv = add_rows(lax.all_gather(kv_weight, 'dp', axis=1, tiled=True))  106 us
    psum x1, blocking collectives, body(): kv_bias_grad = lax.psum(multiply('t,ktc->kc', unit_column, back16), 'dp')  95.7 us
    all_gather x1, waiting for transfers between devices, body(): task_kv = add_rows(lax.all_gather(kv_task, 'dp', axis=1, tiled=True))  91.7 us
    reduce_scatter x1, waiting for transfers between devices, body(): lax.psum_scatter(multiply('td,ktc->dkc', normed_all, back16).astype(jnp.b...  76.6 us
    all_gather x1, waiting for transfers between devices, body(): normed_all = lax.all_gather(normed, 'mp', axis=0, tiled=True)  69.4 us
    unnamed x63, local copies, waits for them, and re-layouts  21.3 us
  transfers between devices with their start and end apart: 4, of which 4 were waited for; matrix products, arithmetic and copies ran while one was open for 11% of the time, Pallas kernels for 0%

commit v1 on v0

--- a/solution.py
+++ b/solution.py
@@ -1,9 +1,429 @@
+import functools
+
 import jax
 import jax.numpy as jnp
 from jax import lax
+from jax.experimental import pallas as pl
+from jax.experimental.pallas import tpu as pltpu
 from jax.sharding import PartitionSpec as P
 
 HEAD = 128
+MESH = pl.DeviceIdType.MESH
+
+
+class Place:
+    def __init__(self):
+        dp = lax.axis_index("dp")
+        self.mp = lax.axis_index("mp")
+        self.z, self.y, self.h = dp // 8, (dp // 2) % 4, dp % 2
+        self.dp = dp
+
+    def index(self, kind, along, across, half):
+        dy, dz = (along, across) if kind == 0 else (across, along)
+        return ((self.z + dz + 4) % 4) * 8 + ((self.y + dy + 4) % 4) * 2 + half
+
+    def device(self, kind, along, across):
+        return (self.index(kind, along, across, self.h), self.mp)
+
+    def partner(self):
+        return (self.dp + 1 - 2 * self.h, self.mp)
+
+    def core_partner(self):
+        return (self.dp, self.mp + 1 - 2 * (self.mp % 2))
+
+    def pair_chip(self):
+        return (self.dp, (self.mp + 2) % 4)
+
+
+def greet(devices):
+    barrier = pltpu.get_barrier_semaphore()
+    for device in devices:
+        pl.semaphore_signal(barrier, inc=1, device_id=device, device_id_type=MESH)
+    pl.semaphore_wait(barrier, len(devices))
+
+
+def ring_devices(place):
+    return [
+        place.device(0, 1, 0),
+        place.device(0, -1, 0),
+        place.device(0, 0, 1),
+        place.device(0, 0, -1),
+        place.partner(),
+    ]
+
+
+class Gather:
+    def __init__(self, place, whole, send, recv):
+        self.place, self.whole, self.send, self.recv = place, whole, send, recv
+        self.slots = [0, 0]
+        self.started = []
+
+    def shard(self, kind, index):
+        return self.whole.at[kind, pl.ds(pl.multiple_of(index * 256, 256), 256), :]
+
+    def copy(self, kind, index, device, slot):
+        block = self.shard(kind, index)
+        return pltpu.make_async_remote_copy(
+            src_ref=block,
+            dst_ref=block,
+            send_sem=self.send.at[kind, slot],
+            recv_sem=self.recv.at[kind, index],
+            device_id=device,
+            device_id_type=MESH,
+        )
+
+    def start(self, kind, index, device):
+        slot = self.slots[kind]
+        self.slots[kind] += 1
+        copy = self.copy(kind, index, device, slot)
+        copy.start()
+        self.started.append(copy)
+
+    def wait(self, kind, index):
+        self.copy(kind, index, self.place.partner(), 0).wait_recv()
+
+    def spread(self, kind, index, along):
+        if along:
+            self.start(kind, index, self.place.device(kind, 1, 0))
+            self.start(kind, index, self.place.device(kind, -1, 0))
+        self.start(kind, index, self.place.device(kind, 0, 1))
+        self.start(kind, index, self.place.device(kind, 0, -1))
+
+    def first(self):
+        own = self.place.dp
+        for kind in range(2):
+            self.start(kind, own, self.place.partner())
+        for kind in range(2):
+            self.spread(kind, own, True)
+
+    def events(self):
+        place = self.place
+
+        def partner(kind):
+            other = place.index(kind, 0, 0, 1 - place.h)
+            self.wait(kind, other)
+            self.spread(kind, other, True)
+
+        def side(kind, along):
+            near, far = (0, 1) if along < 0 else (1, 0)
+            index = place.index(kind, along, 0, near)
+            self.wait(kind, index)
+            self.start(kind, index, place.device(kind, -along, 0))
+            self.spread(kind, index, False)
+            index = place.index(kind, along, 0, far)
+            self.wait(kind, index)
+            self.spread(kind, index, False)
+
+        def opposite(kind):
+            for half in range(2):
+                index = place.index(kind, 2, 0, half)
+                self.wait(kind, index)
+                self.spread(kind, index, False)
+
+        def across(kind, along, step):
+            near, far = (0, 1) if step < 0 else (1, 0)
+            index = place.index(kind, along, step, near)
+            self.wait(kind, index)
+            self.start(kind, index, place.device(kind, 0, -step))
+            self.wait(kind, place.index(kind, along, step, far))
+
+        def across_opposite(kind, along):
+            for half in range(2):
+                self.wait(kind, place.index(kind, along, 2, half))
+
+        result = []
+
+        def add(blocks, function, *rest):
+            for kind in range(2):
+                result.append((kind, blocks, functools.partial(function, kind, *rest)))
+
+        add([(0, 0)], partner)
+        add([(-1, 0)], side, -1)
+        add([(1, 0)], side, 1)
+        add([(0, -1)], across, 0, -1)
+        add([(0, 1)], across, 0, 1)
+        add([(2, 0)], opposite)
+        for along in (-1, 1, 2):
+            add([(along, -1)], across, along, -1)
+            add([(along, 1)], across, along, 1)
+            before = {-1: 0, 1: -1, 2: 1}[along]
+            add([(before, 2)], across_opposite, before)
+        add([(2, 2)], across_opposite, 2)
+        return result
+
+    def finish(self):
+        for copy in self.started:
+            copy.wait_send()
+
+
+GATHER_SEMS = [pltpu.SemaphoreType.DMA((2, 31)), pltpu.SemaphoreType.DMA((2, 32))]
+CHUNK = 32
+
+
+class Rows:
+    def __init__(self, place, whole, send, recv):
+        self.place, self.whole, self.send, self.recv = place, whole, send, recv
+        self.started = []
+
+    def copy(self, owner, chunk, device, lane):
+        rows = pl.multiple_of(owner * 128 + chunk * CHUNK, CHUNK)
+        block = self.whole.at[pl.ds(rows, CHUNK), :]
+        return pltpu.make_async_remote_copy(
+            src_ref=block,
+            dst_ref=block,
+            send_sem=self.send.at[lane, chunk],
+            recv_sem=self.recv.at[owner, chunk],
+            device_id=device,
+            device_id_type=MESH,
+        )
+
+    def start(self, owner, chunk, device, lane):
+        copy = self.copy(owner, chunk, device, lane)
+        copy.start()
+        self.started.append(copy)
+
+    def own(self, chunk):
+        self.start(self.place.mp, chunk, self.place.pair_chip(), 0)
+        self.start(self.place.mp, chunk, self.place.core_partner(), 1)
+
+    def wait(self, owner, chunk):
+        self.copy(owner, chunk, self.place.core_partner(), 0).wait_recv()
+
+    def relay(self, chunk):
+        owner = (self.place.mp + 2) % 4
+        self.wait(owner, chunk)
+        self.start(owner, chunk, self.place.core_partner(), 2)
+
+    def rest(self):
+        mp = self.place.mp
+        other = mp + 1 - 2 * (mp % 2)
+        for chunk in range(128 // CHUNK):
+            self.wait(other, chunk)
+        for chunk in range(128 // CHUNK):
+            self.wait((other + 2) % 4, chunk)
+
+    def finish(self):
+        for copy in self.started:
+            copy.wait_send()
+
+
+ROWS_SEMS = [pltpu.SemaphoreType.DMA((3, 128 // CHUNK)), pltpu.SemaphoreType.DMA((4, 128 // CHUNK))]
+
+
+def gather_kernel(normed, base, task, normed_all, base_all, task_all, *sems):
+    place = Place()
+    local = sems[6]
+    copies = []
+    for at, (source, target) in enumerate(((base, base_all), (task, task_all))):
+        for kind in range(2):
+            block = target.at[kind, pl.ds(pl.multiple_of(place.dp * 256, 256), 256), :]
+            copies.append(pltpu.make_async_copy(source.at[kind], block, local.at[at * 2 + kind]))
+    rows = normed_all.at[pl.ds(pl.multiple_of(place.mp * 128, 128), 128), :]
+    copies.append(pltpu.make_async_copy(normed, rows, local.at[4]))
+    for copy in copies:
+        copy.start()
+    greet(ring_devices(place) + [place.core_partner(), place.pair_chip()])
+    for copy in copies:
+        copy.wait()
+    base_gather = Gather(place, base_all, sems[0], sems[1])
+    task_gather = Gather(place, task_all, sems[2], sems[3])
+    exchange = Rows(place, normed_all, sems[4], sems[5])
+    base_gather.first()
+    for chunk in range(128 // CHUNK):
+        exchange.own(chunk)
+    relays = list(range(128 // CHUNK))
+    for at, (_, _, event) in enumerate(base_gather.events()):
+        event()
+        if at % 8 == 7 and relays:
+            exchange.relay(relays.pop(0))
+    task_gather.first()
+    for at, (_, _, event) in enumerate(task_gather.events()):
+        event()
+        if relays:
+            exchange.relay(relays.pop(0))
+    exchange.rest()
+    base_gather.finish()
+    task_gather.finish()
+    exchange.finish()
+
+
+def gather_all(normed, base, task):
+    any_spec = pl.BlockSpec(memory_space=pl.ANY)
+    return pl.pallas_call(
+        gather_kernel,
+        out_shape=(
+            jax.ShapeDtypeStruct((512, 8192), jnp.bfloat16),
+            jax.ShapeDtypeStruct((2, 8192, 256), jnp.bfloat16),
+            jax.ShapeDtypeStruct((2, 8192, 256), jnp.bfloat16),
+        ),
+        in_specs=[any_spec] * 3,
+        out_specs=(any_spec,) * 3,
+        scratch_shapes=GATHER_SEMS + GATHER_SEMS + ROWS_SEMS + [pltpu.SemaphoreType.DMA((5,))],
+        compiler_params=pltpu.CompilerParams(collective_id=0, has_side_effects=True),
+        name="gather_all",
+    )(normed, base, task)
+
+
+class Scatter:
+    def __init__(self, place, part, land, send, recv):
+        self.place, self.part, self.land, self.send, self.recv = place, part, land, send, recv
+        self.slots = [0, 0]
+        self.started = []
+
+    def own(self, kind, along, across, half):
+        return self.part.at[self.place.index(kind, along, across, half), kind]
+
+    def copy(self, kind, block, spot, device, slot):
+        return pltpu.make_async_remote_copy(
+            src_ref=block,
+            dst_ref=self.land.at[kind, spot],
+            send_sem=self.send.at[kind, slot],
+            recv_sem=self.recv.at[kind, spot],
+            device_id=device,
+            device_id_type=MESH,
+        )
+
+    def start(self, kind, block, spot, device):
+        slot = self.slots[kind]
+        self.slots[kind] += 1
+        copy = self.copy(kind, block, spot, device, slot)
+        copy.start()
+        self.started.append(copy)
+
+    def wait(self, kind, spot):
+        block = self.land.at[kind, spot]
+        self.copy(kind, block, spot, self.place.partner(), 0).wait_recv()
+
+    def add(self, kind, block, spots):
+        for spot in spots:
+            self.wait(kind, spot)
+
+        def step(at, carry):
+            rows = pl.ds(pl.multiple_of(at * 64, 64), 64)
+            total = block[rows, :].astype(jnp.float32)
+            for spot in spots:
+                total = total + self.land[kind, spot, rows, :].astype(jnp.float32)
+            block[rows, :] = total.astype(jnp.bfloat16)
+            return carry
+
+        lax.fori_loop(0, 4, step, 0)
+
+    def first(self, kind):
+        for across in (2, 1, 3, 0):
+            for half, along in ((0, 1), (1, -1)):
+                block = self.own(kind, 2, across, half)
+                self.start(kind, block, half * 4 + across, self.place.device(kind, along, 0))
+
+    def second_own(self, kind):
+        for across in (2, 1, 3, 0):
+            for side, along in ((0, 1), (1, -1)):
+                half = 1 - side
+                block = self.own(kind, along, across, half)
+                spot = 8 + side * 8 + across * 2 + half
+                self.start(kind, block, spot, self.place.device(kind, along, 0))
+
+    def second(self, kind, across):
+        for side, along in ((0, 1), (1, -1)):
+            half = side
+            block = self.own(kind, along, across, half)
+            self.add(kind, block, [side * 4 + across])
+            spot = 8 + side * 8 + across * 2 + half
+            self.start(kind, block, spot, self.place.device(kind, along, 0))
+
+    def third(self, kind, across):
+        for half in range(2):
+            block = self.own(kind, 0, across, half)
+            self.add(kind, block, [8 + across * 2 + half, 16 + across * 2 + half])
+            if across == 2:
+                along = 1 if half == 0 else -1
+                self.start(kind, block, 24 + half, self.place.device(kind, 0, along))
+            if across in (1, 3):
+                side = 0 if across == 1 else 1
+                if half != side:
+                    along = 1 if side == 0 else -1
+                    self.start(kind, block, 26 + side * 2 + half, self.place.device(kind, 0, along))
+
+    def fourth(self, kind):
+        for side, across in ((0, 1), (1, 3)):
+            block = self.own(kind, 0, across, side)
+            self.add(kind, block, [24 + side])
+            along = 1 if side == 0 else -1
+            self.start(kind, block, 26 + side * 2 + side, self.place.device(kind, 0, along))
+
+    def fifth(self, kind):
+        for half in (1 - self.place.h, self.place.h):
+            block = self.own(kind, 0, 0, half)
+            for side in range(2):
+                self.wait(kind, 26 + side * 2 + half)
+
+            def step(at, carry, block=block, half=half):
+                rows = pl.ds(pl.multiple_of(at * 64, 64), 64)
+                total = block[rows, :].astype(jnp.float32)
+                for side in range(2):
+                    total = total + self.land[kind, 26 + side * 2 + half, rows, :].astype(jnp.float32)
+                block[rows, :] = total.astype(jnp.bfloat16)
+                return carry
+
+            lax.fori_loop(0, 4, step, 0)
+            if half is not self.place.h:
+                self.start(kind, block, 30, self.place.partner())
+
+    def last(self, kind, grad):
+        self.wait(kind, 30)
+        block = self.own(kind, 0, 0, self.place.h)
+        total = block[...].astype(jnp.float32) + self.land[kind, 30].astype(jnp.float32)
+        grad[kind] = total.T
+
+    def finish(self):
+        for copy in self.started:
+            copy.wait_send()
+
+
+SCATTER_SCRATCH = [
+    pltpu.VMEM((2, 31, 256, 256), jnp.bfloat16),
+    pltpu.SemaphoreType.DMA((2, 31)),
+    pltpu.SemaphoreType.DMA((2, 31)),
+]
+
+
+def scatter_kernel(given, grad, part, land, send, recv, local):
+    place = Place()
+    load = pltpu.make_async_copy(given, part, local)
+    load.start()
+    greet(ring_devices(place))
+    load.wait()
+    scatter = Scatter(place, part, land, send, recv)
+    for kind in range(2):
+        scatter.first(kind)
+    for kind in range(2):
+        scatter.second_own(kind)
+    for across in (2, 1, 3, 0):
+        for kind in range(2):
+            scatter.second(kind, across)
+    for across in (2, 1, 3, 0):
+        for kind in range(2):
+            scatter.third(kind, across)
+    for kind in range(2):
+        scatter.fourth(kind)
+    for kind in range(2):
+        scatter.fifth(kind)
+    for kind in range(2):
+        scatter.last(kind, grad)
+    scatter.finish()
+
+
+def scatter_all(part):
+    return pl.pallas_call(
+        scatter_kernel,
+        out_shape=jax.ShapeDtypeStruct((2, 256, 256), jnp.float32),
+        in_specs=[pl.BlockSpec(memory_space=pl.ANY)],
+        out_specs=pl.BlockSpec(memory_space=pltpu.VMEM),
+        scratch_shapes=[pltpu.VMEM((32, 2, 256, 256), jnp.bfloat16)] + SCATTER_SCRATCH + [pltpu.SemaphoreType.DMA],
+        compiler_params=pltpu.CompilerParams(
+            collective_id=1, has_side_effects=True, vmem_limit_bytes=40 * 1024 * 1024
+        ),
+        name="scatter_all",
+    )(part)
 
 
 def rotate(field, sign):
@@ -58,7 +478,7 @@
     normed = (
         wide * lax.rsqrt(jnp.mean(wide * wide, axis=-1, keepdims=True) + 1e-06) * gain
     ).astype(jnp.bfloat16)
-    normed_all = lax.all_gather(normed, "mp", axis=0, tiled=True)
+    normed_all, base_rows, task_rows = gather_all(normed, kv_weight, kv_task)
     length = normed_all.shape[0]
     local_width = kv_weight.shape[2]
     local_heads = local_width // HEAD
@@ -66,8 +486,8 @@
     def add_rows(weight_rows):
         return multiply("td,kdc->ktc", normed_all, weight_rows)
 
-    base_kv = add_rows(lax.all_gather(kv_weight, "dp", axis=1, tiled=True))
-    task_kv = add_rows(lax.all_gather(kv_task, "dp", axis=1, tiled=True))
+    base_kv = add_rows(base_rows)
+    task_kv = add_rows(task_rows)
     base_kv = base_kv + kv_bias[:, None, :]
     task_kv = task_kv + kv_bias_task[:, None, :]
     heads_shape = (length, local_heads, HEAD)
@@ -107,13 +527,9 @@
     value_back = jnp.concatenate([item[3] for item in results], axis=1).reshape(length, local_width)
     key_back = rotate(key_turned, -1.0).reshape(length, local_width)
     back16 = jnp.stack([key_back, value_back]).astype(jnp.bfloat16)
-    scattered = lax.psum_scatter(
-        multiply("td,ktc->dkc", normed_all, back16).astype(jnp.bfloat16),
-        "dp",
-        scatter_dimension=0,
-        tiled=True,
-    ).astype(jnp.float32)
-    kv_grad = jnp.transpose(scattered, (1, 0, 2))
+    part = multiply("ktc,td->kcd", back16, normed_all).astype(jnp.bfloat16)
+    part = part.reshape(2, local_width, 32, 256).transpose(2, 0, 1, 3)
+    kv_grad = scatter_all(part)
     unit_column = jnp.ones((length,), jnp.bfloat16)
     kv_bias_grad = lax.psum(multiply("t,ktc->kc", unit_column, back16), "dp")
     return (context, context_tangent, kv_grad, kv_bias_grad)

time: 627 us -> 523 us (0.83)
  waiting for transfers between devices: 344 us -> 0 us
  Pallas kernels: 0 us -> 224 us
  local copies, waits for them, and re-layouts: 26.3 us -> 51.3 us
  between operations: 14.7 us -> 1.28 us
  matrix products: 125 us -> 134 us
    all_gather x3 -> x0, waiting for transfers between devices: 267 us -> none  [the longest x1 106 us: body(): base_kv = add_rows(lax.all_gather(kv_weight, 'dp', axis=1, tiled=True))]
    pallas_call x0 -> x2, Pallas kernels: none -> 224 us  [the longest x1 187 us: gather_all(): pl.pallas_call(gather_kernel, out_shape=(jax.ShapeDtypeStruct((512, 8192)...]
    reduce_scatter x1 -> x0, waiting for transfers between devices: 76.6 us -> none  [body(): lax.psum_scatter(multiply('td,ktc->dkc', normed_all, back16).astype(jnp.b...]
    reshape x0 -> x1, local copies, waits for them, and re-layouts: none -> 11.9 us  [body(): part = part.reshape(2, local_width, 32, 256).transpose(2, 0, 1, 3)]
    convert_element_type x0 -> x1, local copies, waits for them, and re-layouts: none -> 11.9 us  [body(): part = multiply('ktc,td->kcd', back16, normed_all).astype(jnp.bfloat16)]
    dot_general x22, matrix products: 125 us -> 134 us  [multiply(): return jnp.einsum(form, left, right, preferred_element_type=jnp.float32)]
    unnamed x63 -> x36, local copies, waits for them, and re-layouts: 21.3 us -> 24.7 us
  transfers between devices with their start and end apart: 4 -> 0, of which waited for: 4 -> 0; matrix products, arithmetic and copies ran while one was open for 11% -> 0% of each run, Pallas kernels for 0% -> 0%
where the time goes in v1:
time: 523 us; the launch traced here: 515 us
  Pallas kernels  224 us (43%)
  matrix products  134 us (26%)
  blocking collectives  94.1 us (18%)
  local copies, waits for them, and re-layouts  51.3 us (10%)
  other arithmetic  10.3 us (2%)
    pallas_call x1, Pallas kernels, gather_all(): pl.pallas_call(gather_kernel, out_shape=(jax.ShapeDtypeStruct((512, 8192)...  187 us
    dot_general x22, matrix products, multiply(): return jnp.einsum(form, left, right, preferred_element_type=jnp.float32)  134 us
    psum x1, blocking collectives, body(): kv_bias_grad = lax.psum(multiply('t,ktc->kc', unit_column, back16), 'dp')  94.1 us
    pallas_call x1, Pallas kernels, scatter_all(): pl.pallas_call(scatter_kernel, out_shape=jax.ShapeDtypeStruct((2, 256, 25...  37 us
    unnamed x36, local copies, waits for them, and re-layouts  24.7 us
    reshape x1, local copies, waits for them, and re-layouts, body(): part = part.reshape(2, local_width, 32, 256).transpose(2, 0, 1, 3)  11.9 us
    convert_element_type x1, local copies, waits for them, and re-layouts, body(): part = multiply('ktc,td->kcd', back16, normed_all).astype(jnp.bfloat16)  11.9 us

profile of v1, /device:TPU:0, one launch (start us, length us, event | category | flops | bytes accessed | tf_op | source)
XLA Modules:
  0.0 514.6 jit_solution(11169328289305800797)
XLA Ops:
  2.7 3.5 fusion.27.normed
  6.2 186.9 %gather_all.1 = (bf16[512,8192]{1,0:T(8,128)(2,1)}, bf16[2,8192,256]{2,1,0:T(8,128)(2,1)}, bf16[2,8192,256]{2,1,0:T(8,128)(2,1)}) custom-call(bf16[128,8192]{1,0:T(8,128)(2,1)} %fusion.27.normed, bf16[2,256,256]{2,1,0:T(8,128)(2,1)} %base.1, bf16[2,256,256]{2,1,0:T(8,128)(2,1)} %task.1), custom_call_target="tpu_custom_call" | custom-call | tf_op jit(solution)/shard_map/gather_all/pallas_call | solution.py:252
  193.2 9.9 %fusion.76 = f32[2,512,256]{1,2,0:T(8,128)S(1)} fusion(bf16[2,8192,256]{2,1,0:T(8,128)(2,1)} %get-tuple-element.9, bf16[512,8192]{1,0:T(8,128)(2,1)} %get-tuple-element.8, f32[2,256]{1,0:T(2,128)S(1)} %copy-done.9), kind=kOutput, calls=%fused_computation.77 | convolution fusion | flops 4295229440 | bytes 17827840 | tf_op jit(solution)/shard_map/td,kdc->ktc/dot_general | solution.py:444
  204.3 9.9 %fusion.79 = f32[2,512,256]{1,2,0:T(8,128)S(1)} fusion(bf16[2,8192,256]{2,1,0:T(8,128)(2,1)} %get-tuple-element.7, bf16[512,8192]{1,0:T(8,128)(2,1)} %get-tuple-element.8, f32[2,256]{1,0:T(2,128)S(1)} %copy-done.10), kind=kOutput, calls=%fused_computation.78 | convolution fusion | flops 4295229440 | bytes 17827840 | tf_op jit(solution)/shard_map/td,kdc->ktc/dot_general | solution.py:444
  217.5 2.9 copy.47
  220.4 4.4 fusion.113
  224.8 3.0 copy.42
  227.9 8.0 %add_multiply_fusion.1 = f32[512,512,8]{1,0,2:T(8,128)} fusion(f32[512,512,8]{1,0,2:T(8,128)} %fusion.113, bf16[512,2,8,128]{0,3,2,1:T(8,128)(2,1)S(1)} %bitcast.365, bf16[512,2,128]{2,0,1:T(8,128)(2,1)S(1)} %get-tuple-element.28), kind=kOutput, calls=%fused_computation.31 | convolution fusion | flops 541065216 | bytes 17956864 | tf_op jit(solution)/shard_map/tkgh,skh->kgts/dot_general | solution.py:444
  237.1 4.5 add_multiply_fusion
  243.1 3.3 fusion.20
  246.4 3.2 copy-done.5
  252.5 3.9 copy.58
  256.4 5.7 %fusion.115 = f32[512,512,8]{1,0,2:T(8,128)} fusion(bf16[512,2,8,128]{0,3,2,1:T(8,128)(2,1)} %bitcast.379, bf16[512,2,128]{0,2,1:T(8,128)(2,1)S(1)} %bitcast.385), kind=kOutput, calls=%fused_computation.99 | convolution fusion | flops 536870912 | bytes 9568256 | tf_op jit(solution)/shard_map/tkgh,skh->kgts/dot_general | solution.py:444
  262.1 20.5 %fusion.4 = (f32[8,512]{1,0:T(8,128)S(1)}, f32[8,512]{1,0:T(8,128)S(1)}, f32[8,512]{1,0:T(8,128)S(1)}, f32[8,512]{1,0:T(8,128)S(1)}, f32[512,512,8]{1,0,2:T(8,128)}) fusion(f32[8,512]{1,0:T(8,128)S(1)} %get-tuple-element.24, f32[8,512]{1,0:T(8,128)S(1)} %get-tuple-element.37, f32[512,512,8]{1,0,2:T(8,128)} %copy-done.3, ...), kind=kOutput, calls=%fused_computation.11 | convolution fusion | flops 570408960 | bytes 51904512 | tf_op jit(solution)/shard_map/tkgh,skh->kgts/dot_general | solution.py:444
  282.6 7.5 %fusion.94 = f32[512,1,128]{2,0,1:T(8,128)S(1)} fusion(f32[512,512,8]{1,0,2:T(8,128)} %get-tuple-element.40, f32[8,512]{1,0:T(8,128)S(1)} %get-tuple-element.18, bf16[512,2,8,128]{0,3,2,1:T(8,128)(2,1)S(1)} %bitcast.369, f32[512,512,8]{1,0,2:T(8,128)} %copy-done.3, f32[8,512]{1,0:T(8,128)S(1)} %get-tuple-element.24, f32[8,512]{1,0:T(8,128)S(1)} %get-tuple-element.37, ...), kind=kOutput, calls=%fused_computation.83 | convolution fusion | flops 553648128 | bytes 18399232 | tf_op jit(solution)/shard_map/kgts,tkgh->skh/dot_general | solution.py:444
  290.8 5.5 %fusion.97 = f32[512,1,128]{2,0,1:T(8,128)S(1)} fusion(f32[512,512,8]{1,0,2:T(8,128)S(1)} %copy-done.4, f32[8,512]{1,0:T(8,128)S(1)} %get-tuple-element.23, bf16[512,2,8,128]{0,3,2,1:T(8,128)(2,1)S(1)} %bitcast.370, f32[512,512,8]{1,0,2:T(8,128)} %copy-done.5, f32[8,512]{1,0:T(8,128)S(1)} %fusion.22, f32[8,512]{1,0:T(8,128)S(1)} %get-tuple-element.25, ...), kind=kOutput, calls=%fused_computation.84 | convolution fusion | flops 553648128 | bytes 18399232 | tf_op jit(solution)/shard_map/kgts,tkgh->skh/dot_general | solution.py:444
  296.9 6.2 %fusion.106 = bf16[512,1,128]{0,2,1:T(8,128)(2,1)S(1)} fusion(bf16[512,2,8,128]{0,3,2,1:T(8,128)(2,1)} %bitcast.381, f32[512,512,8]{1,0,2:T(8,128)} %copy-done.3, f32[8,512]{1,0:T(8,128)S(1)} %get-tuple-element.24, f32[8,512]{1,0:T(8,128)S(1)} %get-tuple-element.37, pred[512,512]{0,1:T(8,128)(4,1)S(1)} %iota_compare_fusion), kind=kOutput, calls=%fused_computation.87 | convolution fusion | flops 547422208 | bytes 9863168 | tf_op jit(solution)/shard_map/kgts,tkgh->skh/dot_general | solution.py:444
  303.2 4.9 fusion.109
  308.3 94.1 %psum.7 = f32[2,256]{1,0:T(2,128)} all-reduce(f32[2,256]{1,0:T(2,128)S(1)} %bitcast.397), channel_id=1, replica_groups=mesh['dp'=32,'mp'=4] {'dp'}, use_global_device_ids=true, to_apply=%region_9.10 | all-reduce | flops 512 | bytes 4096 | tf_op jit(solution)/shard_map/psum | solution.py:534
  402.4 10.0 %convolution_convert_fusion = bf16[2,256,8192]{2,1,0:T(8,128)(2,1)} fusion(bf16[512,8192]{1,0:T(8,128)(2,1)} %get-tuple-element.8, bf16[1,512,256]{1,2,0:T(8,128)(2,1)S(1)} %bitcast.394, bf16[1,512,256]{1,2,0:T(8,128)(2,1)S(1)} %bitcast.392), kind=kOutput, calls=%fused_computation | convolution fusion | flops 4299423744 | bytes 17301504 | tf_op jit(solution)/shard_map/ktc,td->kcd/dot_general | solution.py:444
  412.4 11.9 %copy.74 = bf16[2,256,8192]{1,2,0:T(8,128)(2,1)} copy(bf16[2,256,8192]{2,1,0:T(8,128)(2,1)} %convolution_convert_fusion) | data formatting | bytes 16777216 | tf_op jit(solution)/shard_map/convert_element_type | solution.py:530
  424.4 11.9 %copy.75 = bf16[2,256,32,256]{3,1,0,2:T(8,128)(2,1)} copy(bf16[2,256,32,256]{1,3,2,0:T(8,128)(2,1)} %bitcast.364) | data formatting | bytes 16777216 | tf_op jit(solution)/shard_map/reshape | solution.py:531
  436.3 3.4 copy-done
  439.7 37.0 %scatter_all.1 = f32[2,256,256]{2,1,0:T(8,128)S(1)} custom-call(bf16[32,2,256,256]{3,2,1,0:T(8,128)(2,1)S(1)} %bitcast.363), custom_call_target="tpu_custom_call" | custom-call | tf_op jit(solution)/shard_map/scatter_all/pallas_call | solution.py:416
  476.7 7.6 %fusion.29 = f32[128,8,512]{2,0,1:T(8,128)S(1)} fusion(f32[512,512,8]{1,0,2:T(8,128)} %add_multiply_fusion.1, f32[8,512]{1,0:T(8,128)S(1)} %get-tuple-element.19, bf16[512,2,128]{0,2,1:T(8,128)(2,1)S(1)} %bitcast.387, f32[512,512,8]{1,0,2:T(8,128)} %copy-done.3, f32[8,512]{1,0:T(8,128)S(1)} %get-tuple-element.24, f32[8,512]{1,0:T(8,128)S(1)} %get-tuple-element.37, ...), kind=kOutput, calls=%fused_computation.46 | convolution fusion | flops 551550976 | bytes 19316736 | tf_op jit(solution)/shard_map/kgts,skh->tkgh/dot_general | solution.py:444
  485.5 2.7 fusion.82
  488.2 5.4 %fusion.32 = f32[128,8,512]{2,0,1:T(8,128)S(1)} fusion(f32[512,512,8]{1,0,2:T(8,128)} %add_multiply_fusion, f32[8,512]{1,0:T(8,128)S(1)} %get-tuple-element.22, bf16[512,2,128]{0,2,1:T(8,128)(2,1)S(1)} %bitcast.388, f32[512,512,8]{1,0,2:T(8,128)S(1)} %bitcast.376, f32[8,512]{1,0:T(8,128)S(1)} %fusion.22, f32[8,512]{1,0:T(8,128)S(1)} %get-tuple-element.25, ...), kind=kOutput, calls=%fused_computation.48 | convolution fusion | flops 551550976 | bytes 19316736 | tf_op jit(solution)/shard_map/kgts,skh->tkgh/dot_general | solution.py:444
  493.7 2.7 fusion.85
  496.6 2.5 copy.77
  499.1 6.0 %fusion.73 = bf16[512,1,8,128]{0,3,2,1:T(8,128)(2,1)S(1)} fusion(bf16[512,2,128]{0,2,1:T(8,128)(2,1)S(1)} %bitcast.389, f32[512,512,8]{1,0,2:T(8,128)} %copy-done.3, f32[8,512]{1,0:T(8,128)S(1)} %get-tuple-element.24, f32[8,512]{1,0:T(8,128)S(1)} %get-tuple-element.37, pred[512,512]{0,1:T(8,128)(4,1)S(1)} %iota_compare_fusion), kind=kOutput, calls=%fused_computation.76 | convolution fusion | flops 547880960 | bytes 9863168 | tf_op jit(solution)/shard_map/kgts,skh->tkgh/dot_general | solution.py:444
  505.1 6.0 %fusion.70 = bf16[512,1,8,128]{0,3,2,1:T(8,128)(2,1)S(1)} fusion(bf16[512,2,128]{0,2,1:T(8,128)(2,1)S(1)} %bitcast.390, f32[512,512,8]{1,0,2:T(8,128)} %copy-done.5, f32[8,512]{1,0:T(8,128)S(1)} %fusion.22, f32[8,512]{1,0:T(8,128)S(1)} %get-tuple-element.25, pred[512,512]{0,1:T(8,128)(4,1)S(1)} %iota_compare_fusion), kind=kOutput, calls=%fused_computation.75 | convolution fusion | flops 547880960 | bytes 9863168 | tf_op jit(solution)/shard_map/kgts,skh->tkgh/dot_general | solution.py:444
  511.3 2.4 copy.76
  (57 shorter events, 15.8 us)
Async XLA Ops:
  0.6 192.5 %copy-start.9 = (f32[2,256]{1,0:T(2,128)S(1)}, f32[2,256]{1,0:T(2,128)}, u32[]{:S(2)}) copy-start(f32[2,256]{1,0:T(2,128)} %param.16) | copy-start | bytes 6148
  193.2 11.1 %copy-start.10 = (f32[2,256]{1,0:T(2,128)S(1)}, f32[2,256]{1,0:T(2,128)}, u32[]{:S(2)}) copy-start(f32[2,256]{1,0:T(2,128)} %param.14) | copy-start | bytes 6148
  203.1 1.0 copy-start.7
  214.3 1.0 copy-start.8
  220.4 4.4 copy-start.1
  227.9 8.0 %copy-start.2 = (bf16[512,2048]{0,1:T(8,128)(2,1)S(1)}, bf16[512,2048]{0,1:T(8,128)(2,1)}, u32[]{:S(2)}) copy-start(bf16[512,2048]{0,1:T(8,128)(2,1)} %copy-done.1) | copy-start | bytes 6291460
  243.1 3.3 copy-start.3
  246.4 3.2 copy-start.5
  282.6 8.2 %copy-start.4 = (f32[512,512,8]{1,0,2:T(8,128)S(1)}, f32[512,512,8]{1,0,2:T(8,128)}, u32[]{:S(2)}) copy-start(f32[512,512,8]{1,0,2:T(8,128)} %fusion.115) | copy-start | bytes 25165828
  296.9 6.2 %copy-start.6 = (bf16[512,2048]{0,1:T(8,128)(2,1)S(1)}, bf16[512,2048]{0,1:T(8,128)(2,1)}, u32[]{:S(2)}) copy-start(bf16[512,2048]{0,1:T(8,128)(2,1)} %copy.58) | copy-start | bytes 6291460
  436.3 3.4 copy-start
  439.7 45.7 %slice-start = ((s8[8388608]{0:T(1024)(128)(4,1)}), s8[4194304]{0:T(1024)(128)(4,1)S(1)}, s32[]{:S(2)}) async-start(s8[8388608]{0:T(1024)(128)(4,1)} %bitcast.373), calls=%async_computation | async-start | bytes 8388608
  439.7 48.5 %slice-start.2 = ((s8[8388608]{0:T(1024)(128)(4,1)}), s8[4194304]{0:T(1024)(128)(4,1)S(1)}, s32[]{:S(2)}) async-start(s8[8388608]{0:T(1024)(128)(4,1)} %bitcast.375), calls=%async_computation.2 | async-start | bytes 8388608
  476.7 8.7 %slice-start.1 = ((s8[8388608]{0:T(1024)(128)(4,1)}), s8[4194304]{0:T(1024)(128)(4,1)S(1)}, s32[]{:S(2)}) async-start(s8[8388608]{0:T(1024)(128)(4,1)} %bitcast.373), calls=%async_computation.1 | async-start | bytes 8388608
  476.7 11.5 %slice-start.3 = ((s8[8388608]{0:T(1024)(128)(4,1)}), s8[4194304]{0:T(1024)(128)(4,1)S(1)}, s32[]{:S(2)}) async-start(s8[8388608]{0:T(1024)(128)(4,1)} %bitcast.375), calls=%async_computation.3 | async-start | bytes 8388608

commit v2 on v1

--- a/solution.py
+++ b/solution.py
@@ -2,6 +2,7 @@
 
 import jax
 import jax.numpy as jnp
+import numpy as np
 from jax import lax
 from jax.experimental import pallas as pl
 from jax.experimental.pallas import tpu as pltpu
@@ -59,7 +60,7 @@
         self.started = []
 
     def shard(self, kind, index):
-        return self.whole.at[kind, pl.ds(pl.multiple_of(index * 256, 256), 256), :]
+        return self.whole.at[kind, index]
 
     def copy(self, kind, index, device, slot):
         block = self.shard(kind, index)
@@ -210,60 +211,6 @@
 ROWS_SEMS = [pltpu.SemaphoreType.DMA((3, 128 // CHUNK)), pltpu.SemaphoreType.DMA((4, 128 // CHUNK))]
 
 
-def gather_kernel(normed, base, task, normed_all, base_all, task_all, *sems):
-    place = Place()
-    local = sems[6]
-    copies = []
-    for at, (source, target) in enumerate(((base, base_all), (task, task_all))):
-        for kind in range(2):
-            block = target.at[kind, pl.ds(pl.multiple_of(place.dp * 256, 256), 256), :]
-            copies.append(pltpu.make_async_copy(source.at[kind], block, local.at[at * 2 + kind]))
-    rows = normed_all.at[pl.ds(pl.multiple_of(place.mp * 128, 128), 128), :]
-    copies.append(pltpu.make_async_copy(normed, rows, local.at[4]))
-    for copy in copies:
-        copy.start()
-    greet(ring_devices(place) + [place.core_partner(), place.pair_chip()])
-    for copy in copies:
-        copy.wait()
-    base_gather = Gather(place, base_all, sems[0], sems[1])
-    task_gather = Gather(place, task_all, sems[2], sems[3])
-    exchange = Rows(place, normed_all, sems[4], sems[5])
-    base_gather.first()
-    for chunk in range(128 // CHUNK):
-        exchange.own(chunk)
-    relays = list(range(128 // CHUNK))
-    for at, (_, _, event) in enumerate(base_gather.events()):
-        event()
-        if at % 8 == 7 and relays:
-            exchange.relay(relays.pop(0))
-    task_gather.first()
-    for at, (_, _, event) in enumerate(task_gather.events()):
-        event()
-        if relays:
-            exchange.relay(relays.pop(0))
-    exchange.rest()
-    base_gather.finish()
-    task_gather.finish()
-    exchange.finish()
-
-
-def gather_all(normed, base, task):
-    any_spec = pl.BlockSpec(memory_space=pl.ANY)
-    return pl.pallas_call(
-        gather_kernel,
-        out_shape=(
-            jax.ShapeDtypeStruct((512, 8192), jnp.bfloat16),
-            jax.ShapeDtypeStruct((2, 8192, 256), jnp.bfloat16),
-            jax.ShapeDtypeStruct((2, 8192, 256), jnp.bfloat16),
-        ),
-        in_specs=[any_spec] * 3,
-        out_specs=(any_spec,) * 3,
-        scratch_shapes=GATHER_SEMS + GATHER_SEMS + ROWS_SEMS + [pltpu.SemaphoreType.DMA((5,))],
-        compiler_params=pltpu.CompilerParams(collective_id=0, has_side_effects=True),
-        name="gather_all",
-    )(normed, base, task)
-
-
 class Scatter:
     def __init__(self, place, part, land, send, recv):
         self.place, self.part, self.land, self.send, self.recv = place, part, land, send, recv
@@ -271,7 +218,7 @@
         self.started = []
 
     def own(self, kind, along, across, half):
-        return self.part.at[self.place.index(kind, along, across, half), kind]
+        return self.part.at[kind, self.place.index(kind, along, across, half)]
 
     def copy(self, kind, block, spot, device, slot):
         return pltpu.make_async_remote_copy(
@@ -379,160 +326,318 @@
             copy.wait_send()
 
 
-SCATTER_SCRATCH = [
-    pltpu.VMEM((2, 31, 256, 256), jnp.bfloat16),
-    pltpu.SemaphoreType.DMA((2, 31)),
-    pltpu.SemaphoreType.DMA((2, 31)),
-]
-
-
-def scatter_kernel(given, grad, part, land, send, recv, local):
+FACTOR = HEAD ** (-0.5)
+EXPONENT = FACTOR * 1.4426950408889634
+F32 = jnp.float32
+BF16 = jnp.bfloat16
+
+
+def product(left, right):
+    return jnp.dot(left, right, preferred_element_type=F32)
+
+
+def product_rows(left, right):
+    return lax.dot_general(left, right, (((1,), (1,)), ((), ())), preferred_element_type=F32)
+
+
+def turn(field, cosine, sine):
+    parts = []
+    for head in range(2):
+        one = field[:, head * HEAD : (head + 1) * HEAD]
+        parts.append(one * cosine + pltpu.roll(one, HEAD // 2, 1) * sine)
+    return jnp.concatenate(parts, axis=1)
+
+
+def softmax_down(keys, queries):
+    scores = product_rows(keys, queries)
+    ahead = lax.broadcasted_iota(jnp.int32, (256, 256), 0) > lax.broadcasted_iota(jnp.int32, (256, 256), 1)
+    own = jnp.where(ahead, -jnp.inf, scores[-256:])
+    scores = own if scores.shape[0] == 256 else jnp.concatenate([scores[:-256], own], axis=0)
+    highest = jnp.max(scores, axis=0, keepdims=True)
+    raised = jnp.exp2((scores - highest) * EXPONENT)
+    return raised * (1.0 / jnp.sum(raised, axis=0, keepdims=True))
+
+
+def columns(head):
+    return pl.ds(pl.multiple_of(head * HEAD, HEAD), HEAD)
+
+
+def base_head(head, query, cotangent, keys, values, key_sum, value_sum):
+    group = head // 8
+    for block in range(2):
+        rows, count = pl.ds(block * 256, 256), (block + 1) * 256
+        queries, pulls = query[rows, columns(head)], cotangent[rows, columns(head)]
+        weights = softmax_down(keys[:count, columns(group)], queries)
+        pulled = product_rows(values[:count, columns(group)], pulls)
+        mean = jnp.sum(weights * pulled, axis=0, keepdims=True)
+        back = (weights * (pulled - mean) * FACTOR).astype(BF16)
+        value_sum[:count, columns(group)] += product(weights.astype(BF16), pulls)
+        key_sum[:count, columns(group)] += product(back, queries)
+
+
+def tangent_head(head, query, tangent, keys, key_tangent, turned, context, context_tangent):
+    group = head // 8
+    for block in range(2):
+        rows, count = pl.ds(block * 256, 256), (block + 1) * 256
+        queries = query[rows, columns(head)]
+        weights = softmax_down(keys[:count, columns(group)], queries)
+        both_keys = jnp.concatenate([keys[:count, columns(group)], key_tangent[:count, columns(group)]], axis=1)
+        both_queries = jnp.concatenate([tangent[rows, columns(head)], queries], axis=1)
+        spread = product_rows(both_keys, both_queries)
+        mean = jnp.sum(weights * spread, axis=0, keepdims=True)
+        moved = (weights * (spread - mean) * FACTOR).astype(BF16)
+        first = product(turned[group, :, :count], weights.astype(BF16))
+        second = product(turned[group, :HEAD, :count], moved)
+        context[rows, columns(head)] = first[:HEAD].T.astype(BF16)
+        context_tangent[rows, columns(head)] = (first[HEAD:] + second).T.astype(BF16)
+
+
+def project(normed, whole, bias, total):
+    total[...] = jnp.zeros_like(total) + jnp.concatenate([bias[0:1, :], bias[1:2, :]], axis=1)
+
+    def step(at, carry):
+        for kind in range(2):
+            sums = 0.0
+            for part in range(4):
+                index = at * 4 + part
+                left = normed[:, pl.ds(pl.multiple_of(index * 256, 256), 256)]
+                sums = sums + product(left, whole[kind, index])
+            total[:, kind * 256 : (kind + 1) * 256] += sums
+        return carry
+
+    lax.fori_loop(0, 8, step, 0)
+
+
+def layer_kernel(
+    tokens, gain, query_in, tangent_in, kv_in, bias, task_in, bias_task, cotangent_in, cosine, sine,
+    context, context_tangent, grad, bias_grad,
+    token_rows, query, tangent, cotangent, normed, base_all, task_all, land, total,
+    keys, values, key_tangent, value_tangent, turned, key_sum, value_sum, back, sums, sums_land,
+    local, base_send, base_recv, task_send, task_recv, rows_send, rows_recv,
+    part_send, part_recv, sums_send, sums_recv,
+):
     place = Place()
-    load = pltpu.make_async_copy(given, part, local)
-    load.start()
-    greet(ring_devices(place))
-    load.wait()
-    scatter = Scatter(place, part, land, send, recv)
+
+    def load(source, target, at):
+        copy = pltpu.make_async_copy(source, target, local.at[at])
+        copy.start()
+        return copy
+
+    waits = []
+    for kind in range(2):
+        waits.append(load(kv_in.at[kind], base_all.at[kind, place.dp], kind))
+        waits.append(load(task_in.at[kind], task_all.at[kind, place.dp], 2 + kind))
+    waits.append(load(tokens, token_rows, 4))
+    later = [load(query_in, query, 5), load(cotangent_in, cotangent, 6), load(tangent_in, tangent, 7)]
+    greet(ring_devices(place) + [place.core_partner(), place.pair_chip()])
+    for copy in waits:
+        copy.wait()
+    base = Gather(place, base_all, base_send, base_recv)
+    task = Gather(place, task_all, task_send, task_recv)
+    rows = Rows(place, normed, rows_send, rows_recv)
+    base.first()
+
+    scale = gain[...]
+    for chunk in range(128 // CHUNK):
+
+        def norm(at, carry, chunk=chunk):
+            here = pl.multiple_of(chunk * CHUNK + at * 16, 16)
+            wide = token_rows[pl.ds(here, 16), :].astype(F32)
+            mean = jnp.mean(wide * wide, axis=-1, keepdims=True)
+            there = pl.multiple_of(place.mp * 128 + here, 16)
+            normed[pl.ds(there, 16), :] = (wide * lax.rsqrt(mean + 1e-06) * scale).astype(BF16)
+            return carry
+
+        lax.fori_loop(0, CHUNK // 16, norm, 0)
+        rows.own(chunk)
+    for copy in later:
+        copy.wait()
+
+    relays = list(range(128 // CHUNK))
+    for at, (_, _, event) in enumerate(base.events()):
+        event()
+        if at in (12, 18, 23):
+            rows.relay(relays.pop(0))
+    task.first()
+    for chunk in relays:
+        rows.relay(chunk)
+    rows.rest()
+    ahead = [event for _, _, event in task.events()]
+
+    def events(count):
+        for _ in range(min(count, len(ahead))):
+            ahead.pop(0)()
+
+    project(normed, base_all, bias, total)
+    events(4)
+    keys[...] = turn(total[:, :256], cosine[...], sine[...]).astype(BF16)
+    values[...] = total[:, 256:].astype(BF16)
+    key_sum[...] = jnp.zeros_like(key_sum)
+    value_sum[...] = jnp.zeros_like(value_sum)
+    for quarter in range(4):
+
+        def base_step(at, carry, quarter=quarter):
+            base_head(quarter * 4 + at, query, cotangent, keys, values, key_sum, value_sum)
+            return carry
+
+        lax.fori_loop(0, 4, base_step, 0)
+        events(4)
+
+    key_back = turn(key_sum[...], cosine[...], -sine[...]).astype(BF16)
+    value_back = value_sum[...].astype(BF16)
+    back[:256, :] = key_back.astype(F32).T.astype(BF16)
+    back[256:, :] = value_back.astype(F32).T.astype(BF16)
+    sums[0] = jnp.zeros_like(sums[0])
+    sums[0, 0:1, :] = jnp.sum(key_back.astype(F32), axis=0, keepdims=True)
+    sums[0, 1:2, :] = jnp.sum(value_back.astype(F32), axis=0, keepdims=True)
+    base.finish()
+
+    def grad_step(at, carry):
+        block = product(back[...], normed[:, pl.ds(pl.multiple_of(at * 256, 256), 256)]).astype(BF16)
+        base_all[0, at] = block[:256]
+        base_all[1, at] = block[256:]
+        return carry
+
+    lax.fori_loop(0, 32, grad_step, 0)
+    scatter = Scatter(place, base_all, land, part_send, part_recv)
+
+    odd_y, odd_z = place.y % 2, place.z % 2
+    mates = [
+        place.device(0, 1 - 2 * odd_y, 0),
+        place.device(0, 2 * odd_y - 1, 0),
+        place.device(1, 1 - 2 * odd_z, 0),
+        place.device(1, 2 * odd_z - 1, 0),
+        place.partner(),
+    ]
+
+    def mate_copy(at):
+        return pltpu.make_async_remote_copy(
+            src_ref=sums.at[at],
+            dst_ref=sums_land.at[at],
+            send_sem=sums_send.at[at],
+            recv_sem=sums_recv.at[at],
+            device_id=mates[at],
+            device_id_type=MESH,
+        )
+
+    def mate_sum(at):
+        mate_copy(at).wait()
+        sums[at + 1] = sums[at] + sums_land[at]
+        if at + 1 < 5:
+            mate_copy(at + 1).start()
+
+    events(len(ahead))
     for kind in range(2):
         scatter.first(kind)
     for kind in range(2):
         scatter.second_own(kind)
-    for across in (2, 1, 3, 0):
+    mate_copy(0).start()
+    project(normed, task_all, bias_task, total)
+    key_tangent[...] = turn(total[:, :256], cosine[...], sine[...]).astype(BF16)
+    value_tangent[...] = total[:, 256:].astype(BF16)
+    for group in range(2):
+        pick = slice(group * HEAD, (group + 1) * HEAD)
+        turned[group, :HEAD, :] = values[:, pick].astype(F32).T.astype(BF16)
+        turned[group, HEAD:, :] = value_tangent[:, pick].astype(F32).T.astype(BF16)
+
+    def tangents(start, count):
+        def step(at, carry):
+            tangent_head(start + at, query, tangent, keys, key_tangent, turned, context, context_tangent)
+            return carry
+
+        lax.fori_loop(0, count, step, 0)
+
+    for at, across in enumerate((2, 1, 3, 0)):
+        mate_sum(at)
         for kind in range(2):
             scatter.second(kind, across)
+        if at % 2 == 1:
+            tangents(at // 2 * 4, 4)
+    mate_sum(4)
     for across in (2, 1, 3, 0):
         for kind in range(2):
             scatter.third(kind, across)
+    tangents(8, 4)
     for kind in range(2):
         scatter.fourth(kind)
+    tangents(12, 4)
     for kind in range(2):
         scatter.fifth(kind)
     for kind in range(2):
         scatter.last(kind, grad)
+    bias_grad[...] = sums[5, 0:2, :]
     scatter.finish()
-
-
-def scatter_all(part):
+    task.finish()
+    rows.finish()
+
+
+def layer(*operands):
+    vmem = pl.BlockSpec(memory_space=pltpu.VMEM)
+    hbm = pl.BlockSpec(memory_space=pl.ANY)
+    scratch = [
+        pltpu.VMEM((128, 8192), BF16),
+        pltpu.VMEM((512, 2048), BF16),
+        pltpu.VMEM((512, 2048), BF16),
+        pltpu.VMEM((512, 2048), BF16),
+        pltpu.VMEM((512, 8192), BF16),
+        pltpu.VMEM((2, 32, 256, 256), BF16),
+        pltpu.VMEM((2, 32, 256, 256), BF16),
+        pltpu.VMEM((2, 31, 256, 256), BF16),
+        pltpu.VMEM((512, 512), F32),
+        pltpu.VMEM((512, 256), BF16),
+        pltpu.VMEM((512, 256), BF16),
+        pltpu.VMEM((512, 256), BF16),
+        pltpu.VMEM((512, 256), BF16),
+        pltpu.VMEM((2, 256, 512), BF16),
+        pltpu.VMEM((512, 256), F32),
+        pltpu.VMEM((512, 256), F32),
+        pltpu.VMEM((512, 512), BF16),
+        pltpu.VMEM((6, 8, 256), F32),
+        pltpu.VMEM((5, 8, 256), F32),
+        pltpu.SemaphoreType.DMA((8,)),
+        *GATHER_SEMS,
+        *GATHER_SEMS,
+        *ROWS_SEMS,
+        pltpu.SemaphoreType.DMA((2, 31)),
+        pltpu.SemaphoreType.DMA((2, 31)),
+        pltpu.SemaphoreType.DMA((5,)),
+        pltpu.SemaphoreType.DMA((5,)),
+    ]
     return pl.pallas_call(
-        scatter_kernel,
-        out_shape=jax.ShapeDtypeStruct((2, 256, 256), jnp.float32),
-        in_specs=[pl.BlockSpec(memory_space=pl.ANY)],
-        out_specs=pl.BlockSpec(memory_space=pltpu.VMEM),
-        scratch_shapes=[pltpu.VMEM((32, 2, 256, 256), jnp.bfloat16)] + SCATTER_SCRATCH + [pltpu.SemaphoreType.DMA],
+        layer_kernel,
+        out_shape=(
+            jax.ShapeDtypeStruct((512, 2048), BF16),
+            jax.ShapeDtypeStruct((512, 2048), BF16),
+            jax.ShapeDtypeStruct((2, 256, 256), F32),
+            jax.ShapeDtypeStruct((2, 256), F32),
+        ),
+        in_specs=[hbm, vmem, hbm, hbm, hbm, vmem, hbm, vmem, hbm, vmem, vmem],
+        out_specs=(vmem,) * 4,
+        scratch_shapes=scratch,
         compiler_params=pltpu.CompilerParams(
-            collective_id=1, has_side_effects=True, vmem_limit_bytes=40 * 1024 * 1024
+            collective_id=0, has_side_effects=True, vmem_limit_bytes=62 * 1024 * 1024
         ),
-        name="scatter_all",
-    )(part)
-
-
-def rotate(field, sign):
-    length = field.shape[0]
-    width = field.shape[-1]
-    half_width = width // 2
-    position = jnp.arange(length).astype(jnp.float32)
-    frequency = jnp.power(1000000.0, -2.0 * jnp.arange(half_width).astype(jnp.float32) / width)
-    angle = position[:, None] * frequency[None, :]
-    angle = jnp.concatenate([angle, angle], axis=-1)
-    cosine = jnp.cos(angle)[:, None, :]
-    sine = sign * jnp.sin(angle)[:, None, :]
-    turned = jnp.concatenate([-field[..., half_width:], field[..., :half_width]], axis=-1)
-    return field * cosine + turned * sine
-
-
-def multiply(form, left, right):
-    return jnp.einsum(form, left, right, preferred_element_type=jnp.float32)
-
-
-def attend(queries, query_tangent, cotangent, keys, values, key_tangent, value_tangent):
-    factor = HEAD ** (-0.5)
-    length = queries.shape[0]
-    causal = jnp.arange(length)[:, None] >= jnp.arange(length)[None, :]
-    scores = multiply("tkgh,skh->kgts", queries, keys) * factor
-    scores = jnp.where(causal, scores, -jnp.inf)
-    highest = jnp.max(scores, axis=-1, keepdims=True)
-    raised = jnp.exp(scores - highest)
-    weights = raised / jnp.sum(raised, axis=-1, keepdims=True)
-    weights16 = weights.astype(jnp.bfloat16)
-    context = multiply("kgts,skh->tkgh", weights16, values)
-    spread = (
-        multiply("tkgh,skh->kgts", query_tangent, keys)
-        + multiply("tkgh,skh->kgts", queries, key_tangent)
-    ) * factor
-    moved = weights * (spread - jnp.sum(weights * spread, axis=-1, keepdims=True))
-    moved16 = moved.astype(jnp.bfloat16)
-    context_tangent = multiply("kgts,skh->tkgh", moved16, values) + multiply(
-        "kgts,skh->tkgh", weights16, value_tangent
+        name="layer",
+    )(*operands)
+
+
+def turning_tables():
+    position = np.arange(512, dtype=np.float64)[:, None]
+    frequency = 1000000.0 ** (-2.0 * np.arange(64) / 128)
+    angle = position * frequency[None, :]
+    cosine, sine = np.cos(angle), np.sin(angle)
+    return (
+        np.concatenate([cosine, cosine], axis=1).astype(np.float32),
+        np.concatenate([-sine, sine], axis=1).astype(np.float32),
     )
-    value_back = multiply("kgts,tkgh->skh", weights16, cotangent)
-    pulled = multiply("tkgh,skh->kgts", cotangent, values)
-    score_back = (
-        weights * (pulled - jnp.sum(weights * pulled, axis=-1, keepdims=True)) * factor
-    ).astype(jnp.bfloat16)
-    key_turned = multiply("kgts,tkgh->skh", score_back, queries)
-    return (context, context_tangent, key_turned, value_back)
 
 
 def body(tokens, gain, query, query_tangent, kv_weight, kv_bias, kv_task, kv_bias_task, cotangent):
-    wide = tokens.astype(jnp.float32)
-    normed = (
-        wide * lax.rsqrt(jnp.mean(wide * wide, axis=-1, keepdims=True) + 1e-06) * gain
-    ).astype(jnp.bfloat16)
-    normed_all, base_rows, task_rows = gather_all(normed, kv_weight, kv_task)
-    length = normed_all.shape[0]
-    local_width = kv_weight.shape[2]
-    local_heads = local_width // HEAD
-
-    def add_rows(weight_rows):
-        return multiply("td,kdc->ktc", normed_all, weight_rows)
-
-    base_kv = add_rows(base_rows)
-    task_kv = add_rows(task_rows)
-    base_kv = base_kv + kv_bias[:, None, :]
-    task_kv = task_kv + kv_bias_task[:, None, :]
-    heads_shape = (length, local_heads, HEAD)
-    keys = rotate(base_kv[0].reshape(heads_shape), 1.0).astype(jnp.bfloat16)
-    values = base_kv[1].reshape(heads_shape).astype(jnp.bfloat16)
-    key_tangent = rotate(task_kv[0].reshape(heads_shape), 1.0).astype(jnp.bfloat16)
-    value_tangent = task_kv[1].reshape(heads_shape).astype(jnp.bfloat16)
-    grouped = (length, local_heads, -1, HEAD)
-    queries = query.reshape(grouped)
-    tangents = query_tangent.reshape(grouped)
-    cotangents = cotangent.reshape(grouped)
-    results = []
-    for head_index in range(local_heads):
-        pick = slice(head_index, head_index + 1)
-        results.append(
-            attend(
-                queries[:, pick],
-                tangents[:, pick],
-                cotangents[:, pick],
-                keys[:, pick],
-                values[:, pick],
-                key_tangent[:, pick],
-                value_tangent[:, pick],
-            )
-        )
-    context = (
-        jnp.concatenate([item[0] for item in results], axis=1)
-        .reshape(length, -1)
-        .astype(jnp.bfloat16)
+    cosine, sine = turning_tables()
+    return layer(
+        tokens, gain.reshape(1, -1), query, query_tangent, kv_weight, kv_bias, kv_task, kv_bias_task, cotangent,
+        jnp.asarray(cosine), jnp.asarray(sine),
     )
-    context_tangent = (
-        jnp.concatenate([item[1] for item in results], axis=1)
-        .reshape(length, -1)
-        .astype(jnp.bfloat16)
-    )
-    key_turned = jnp.concatenate([item[2] for item in results], axis=1)
-    value_back = jnp.concatenate([item[3] for item in results], axis=1).reshape(length, local_width)
-    key_back = rotate(key_turned, -1.0).reshape(length, local_width)
-    back16 = jnp.stack([key_back, value_back]).astype(jnp.bfloat16)
-    part = multiply("ktc,td->kcd", back16, normed_all).astype(jnp.bfloat16)
-    part = part.reshape(2, local_width, 32, 256).transpose(2, 0, 1, 3)
-    kv_grad = scatter_all(part)
-    unit_column = jnp.ones((length,), jnp.bfloat16)
-    kv_bias_grad = lax.psum(multiply("t,ktc->kc", unit_column, back16), "dp")
-    return (context, context_tangent, kv_grad, kv_bias_grad)
 
 
 def solution(mesh):

time: 523 us -> 189 us (0.36); the launches traced: 515 us -> 188 us
  matrix products: 134 us -> 0 us
  blocking collectives: 94.1 us -> 0 us
  local copies, waits for them, and re-layouts: 51.3 us -> 6.06 us
  Pallas kernels: 224 us -> 181 us
  other arithmetic: 10.3 us -> 0 us
    dot_general x22 -> x0, matrix products: 134 us -> none  [multiply(): return jnp.einsum(form, left, right, preferred_element_type=jnp.float32)]
    psum x1 -> x0, blocking collectives: 94.1 us -> none  [body(): kv_bias_grad = lax.psum(multiply('t,ktc->kc', unit_column, back16), 'dp')]
    pallas_call x2 -> x1, Pallas kernels: 224 us -> 181 us  [layer(): pl.pallas_call(layer_kernel, out_shape=(jax.ShapeDtypeStruct((512, 2048),...]
    unnamed x36 -> x10, local copies, waits for them, and re-layouts: 24.7 us -> 6.06 us
    reshape x1 -> x0, local copies, waits for them, and re-layouts: 11.9 us -> none  [body(): part = part.reshape(2, local_width, 32, 256).transpose(2, 0, 1, 3)]
    convert_element_type x1 -> x0, local copies, waits for them, and re-layouts: 11.9 us -> none  [body(): part = multiply('ktc,td->kcd', back16, normed_all).astype(jnp.bfloat16)]
where the time goes in v2:
time: 189 us; the launch traced here: 188 us
  Pallas kernels  181 us (96%)
  local copies, waits for them, and re-layouts  6.06 us (3%)
    pallas_call x1, Pallas kernels, layer(): pl.pallas_call(layer_kernel, out_shape=(jax.ShapeDtypeStruct((512, 2048),...  181 us
    unnamed x10, local copies, waits for them, and re-layouts  6.06 us

profile of v2, /device:TPU:0, one launch (start us, length us, event | category | flops | bytes accessed | tf_op | source)
XLA Modules:
  0.0 188.0 jit_solution(10132171476124582806)
XLA Ops:
  0.6 181.3 %layer.1 = (bf16[512,2048]{1,0:T(8,128)(2,1)}, bf16[512,2048]{1,0:T(8,128)(2,1)}, f32[2,256,256]{2,1,0:T(8,128)}, f32[2,256]{1,0:T(2,128)}) custom-call(bf16[128,8192]{1,0:T(8,128)(2,1)} %tokens.1, f32[1,8192]{1,0:T(1,128)} %bitcast.1, bf16[512,2048]{1,0:T(8,128)(2,1)} %query_in.1, bf16[512,2048]{1,0:T(8,128)(2,1)} %tangent_in.1, ...), custom_call_target="tpu_custom_call" | custom-call | tf_op jit(solution)/shard_map/layer/pallas_call | solution.py:606
  181.9 0.0 copy-start
  181.9 3.3 %copy.19 = bf16[512,2048]{1,0:T(8,128)(2,1)} copy(bf16[512,2048]{1,0:T(8,128)(2,1)} %get-tuple-element.8) | data formatting | bytes 4194304
  185.2 0.0 copy-done
  185.2 0.0 copy-start.1
  185.2 0.0 copy-start.2
  185.2 1.3 copy.20
  186.6 0.1 copy-done.1
  186.6 0.8 copy.21
  187.4 0.0 copy-done.2
  187.4 0.6 copy.22
Async XLA Ops:
  181.9 3.3 %copy-start = (bf16[512,2048]{1,0:T(8,128)(2,1)S(1)}, bf16[512,2048]{1,0:T(8,128)(2,1)}, u32[]{:S(2)}) copy-start(bf16[512,2048]{1,0:T(8,128)(2,1)} %get-tuple-element.9) | copy-start | bytes 6291460
  185.2 1.4 copy-start.1
  185.2 2.2 %copy-start.2 = (f32[2,256]{1,0:T(2,128)S(1)}, f32[2,256]{1,0:T(2,128)}, u32[]{:S(2)}) copy-start(f32[2,256]{1,0:T(2,128)} %get-tuple-element.11) | copy-start | bytes 6148

commit v3 on v2

--- a/solution.py
+++ b/solution.py
@@ -34,6 +34,14 @@
 
     def pair_chip(self):
         return (self.dp, (self.mp + 2) % 4)
+
+    def other_block(self):
+        x = (self.h * 2 + self.mp // 2 + 2 * (self.mp // 2) + 3) % 4
+        return x * 2 + self.mp % 2
+
+    def other_chip(self):
+        block = self.other_block()
+        return (self.dp - self.h + block // 4, block % 4)
 
 
 def greet(devices):
@@ -54,18 +62,16 @@
 
 
 class Gather:
-    def __init__(self, place, whole, send, recv):
-        self.place, self.whole, self.send, self.recv = place, whole, send, recv
+    def __init__(self, place, piece, partner_piece, send, recv):
+        self.place, self.piece, self.partner_piece = place, piece, partner_piece
+        self.send, self.recv = send, recv
         self.slots = [0, 0]
         self.started = []
 
-    def shard(self, kind, index):
-        return self.whole.at[kind, index]
-
-    def copy(self, kind, index, device, slot):
-        block = self.shard(kind, index)
+    def copy(self, kind, index, device, slot, source=None):
+        block = self.piece(kind, index)
         return pltpu.make_async_remote_copy(
-            src_ref=block,
+            src_ref=block if source is None else source,
             dst_ref=block,
             send_sem=self.send.at[kind, slot],
             recv_sem=self.recv.at[kind, index],
@@ -73,10 +79,10 @@
             device_id_type=MESH,
         )
 
-    def start(self, kind, index, device):
+    def start(self, kind, index, device, source=None):
         slot = self.slots[kind]
         self.slots[kind] += 1
-        copy = self.copy(kind, index, device, slot)
+        copy = self.copy(kind, index, device, slot, source)
         copy.start()
         self.started.append(copy)
 
@@ -93,7 +99,7 @@
     def first(self):
         own = self.place.dp
         for kind in range(2):
-            self.start(kind, own, self.place.partner())
+            self.start(kind, own, self.place.partner(), self.partner_piece(kind))
         for kind in range(2):
             self.spread(kind, own, True)
 
@@ -164,6 +170,12 @@
 class Rows:
     def __init__(self, place, whole, send, recv):
         self.place, self.whole, self.send, self.recv = place, whole, send, recv
+        mp, h = place.mp, place.h
+        self.mine = h * 4 + mp
+        self.pair = h * 4 + (mp + 2) % 4
+        self.other = place.other_block()
+        x = (h * 2 + mp // 2 + 2) % 4
+        self.far = x * 2 + mp % 2
         self.started = []
 
     def copy(self, owner, chunk, device, lane):
@@ -184,31 +196,39 @@
         self.started.append(copy)
 
     def own(self, chunk):
-        self.start(self.place.mp, chunk, self.place.pair_chip(), 0)
-        self.start(self.place.mp, chunk, self.place.core_partner(), 1)
+        self.start(self.mine, chunk, self.place.pair_chip(), 0)
+        self.start(self.mine, chunk, self.place.other_chip(), 1)
+        self.start(self.mine, chunk, self.place.core_partner(), 2)
 
     def wait(self, owner, chunk):
         self.copy(owner, chunk, self.place.core_partner(), 0).wait_recv()
 
+    def arrive(self, chunk):
+        for owner, lane in ((self.pair, 3), (self.other, 4)):
+            self.wait(owner, chunk)
+            self.start(owner, chunk, self.place.core_partner(), lane)
+
     def relay(self, chunk):
-        owner = (self.place.mp + 2) % 4
-        self.wait(owner, chunk)
-        self.start(owner, chunk, self.place.core_partner(), 2)
-
-    def rest(self):
-        mp = self.place.mp
-        other = mp + 1 - 2 * (mp % 2)
-        for chunk in range(128 // CHUNK):
-            self.wait(other, chunk)
-        for chunk in range(128 // CHUNK):
-            self.wait((other + 2) % 4, chunk)
+        if chunk < 128 // CHUNK // 2:
+            self.start(self.pair, chunk, self.place.other_chip(), 5)
+        else:
+            self.start(self.other, chunk, self.place.pair_chip(), 5)
+
+    def arrive_far(self, chunk):
+        self.wait(self.far, chunk)
+        self.start(self.far, chunk, self.place.core_partner(), 6)
+
+    def rest(self, owners):
+        for owner in owners:
+            for chunk in range(128 // CHUNK):
+                self.wait(owner + 1 - 2 * (owner % 2), chunk)
 
     def finish(self):
         for copy in self.started:
             copy.wait_send()
 
 
-ROWS_SEMS = [pltpu.SemaphoreType.DMA((3, 128 // CHUNK)), pltpu.SemaphoreType.DMA((4, 128 // CHUNK))]
+ROWS_SEMS = [pltpu.SemaphoreType.DMA((7, 128 // CHUNK)), pltpu.SemaphoreType.DMA((8, 128 // CHUNK))]
 
 
 class Scatter:
@@ -218,7 +238,7 @@
         self.started = []
 
     def own(self, kind, along, across, half):
-        return self.part.at[kind, self.place.index(kind, along, across, half)]
+        return self.part.at[self.place.index(kind, along, across, half), pl.ds(kind * 128, 128), :]
 
     def copy(self, kind, block, spot, device, slot):
         return pltpu.make_async_remote_copy(
@@ -253,7 +273,7 @@
             block[rows, :] = total.astype(jnp.bfloat16)
             return carry
 
-        lax.fori_loop(0, 4, step, 0)
+        lax.fori_loop(0, 2, step, 0)
 
     def first(self, kind):
         for across in (2, 1, 3, 0):
@@ -297,29 +317,25 @@
             along = 1 if side == 0 else -1
             self.start(kind, block, 26 + side * 2 + side, self.place.device(kind, 0, along))
 
-    def fifth(self, kind):
+    def fifth(self, kind, grad):
         for half in (1 - self.place.h, self.place.h):
-            block = self.own(kind, 0, 0, half)
             for side in range(2):
                 self.wait(kind, 26 + side * 2 + half)
-
-            def step(at, carry, block=block, half=half):
-                rows = pl.ds(pl.multiple_of(at * 64, 64), 64)
-                total = block[rows, :].astype(jnp.float32)
-                for side in range(2):
-                    total = total + self.land[kind, 26 + side * 2 + half, rows, :].astype(jnp.float32)
-                block[rows, :] = total.astype(jnp.bfloat16)
-                return carry
-
-            lax.fori_loop(0, 4, step, 0)
-            if half is not self.place.h:
-                self.start(kind, block, 30, self.place.partner())
+        block = self.own(kind, 0, 0, 1 - self.place.h)
+        block[...] = self.summed(kind, 1 - self.place.h).astype(jnp.bfloat16)
+        self.start(kind, block, 30, self.place.partner())
+        grad[self.place.h, :, kind * 128 : (kind + 1) * 128] = self.summed(kind, self.place.h).T
+
+    def summed(self, kind, half):
+        total = self.own(kind, 0, 0, half)[...].astype(jnp.float32)
+        for side in range(2):
+            total = total + self.land[kind, 26 + side * 2 + half].astype(jnp.float32)
+        return total
 
     def last(self, kind, grad):
         self.wait(kind, 30)
-        block = self.own(kind, 0, 0, self.place.h)
-        total = block[...].astype(jnp.float32) + self.land[kind, 30].astype(jnp.float32)
-        grad[kind] = total.T
+        block = self.land[kind, 30].astype(jnp.float32)
+        grad[1 - self.place.h, :, kind * 128 : (kind + 1) * 128] = block.T
 
     def finish(self):
         for copy in self.started:
@@ -392,16 +408,16 @@
         context_tangent[rows, columns(head)] = (first[HEAD:] + second).T.astype(BF16)
 
 
-def project(normed, whole, bias, total):
-    total[...] = jnp.zeros_like(total) + jnp.concatenate([bias[0:1, :], bias[1:2, :]], axis=1)
+def project(normed, start, weights, total):
+    total[...] = jnp.zeros_like(total)
 
     def step(at, carry):
-        for kind in range(2):
+        for kind, weight in enumerate(weights):
             sums = 0.0
             for part in range(4):
                 index = at * 4 + part
-                left = normed[:, pl.ds(pl.multiple_of(index * 256, 256), 256)]
-                sums = sums + product(left, whole[kind, index])
+                left = normed[pl.ds(start, 512), pl.ds(pl.multiple_of(index * 256, 256), 256)]
+                sums = sums + product(left, weight[index])
             total[:, kind * 256 : (kind + 1) * 256] += sums
         return carry
 
@@ -411,29 +427,39 @@
 def layer_kernel(
     tokens, gain, query_in, tangent_in, kv_in, bias, task_in, bias_task, cotangent_in, cosine, sine,
     context, context_tangent, grad, bias_grad,
-    token_rows, query, tangent, cotangent, normed, base_all, task_all, land, total,
-    keys, values, key_tangent, value_tangent, turned, key_sum, value_sum, back, sums, sums_land,
+    token_rows, query, tangent, cotangent, normed, base_all, task_own, task_all, part, land, total, task_total,
+    keys, values, kv_tangent, tangent_out, turned, key_sum, value_sum, back, back_kind, sums, sums_land,
     local, base_send, base_recv, task_send, task_recv, rows_send, rows_recv,
-    part_send, part_recv, sums_send, sums_recv,
+    part_send, part_recv, sums_send, sums_recv, pass_send, pass_recv,
 ):
     place = Place()
+    h = place.h
 
     def load(source, target, at):
         copy = pltpu.make_async_copy(source, target, local.at[at])
         copy.start()
         return copy
 
-    waits = []
-    for kind in range(2):
-        waits.append(load(kv_in.at[kind], base_all.at[kind, place.dp], kind))
-        waits.append(load(task_in.at[kind], task_all.at[kind, place.dp], 2 + kind))
+    waits = [load(kv_in.at[kind], base_all.at[kind, place.dp], kind) for kind in range(2)]
+    waits.append(load(task_in, task_own, 2))
+    waits.append(load(task_in.at[h], task_all.at[place.dp], 3))
     waits.append(load(tokens, token_rows, 4))
     later = [load(query_in, query, 5), load(cotangent_in, cotangent, 6), load(tangent_in, tangent, 7)]
-    greet(ring_devices(place) + [place.core_partner(), place.pair_chip()])
+    greet(ring_devices(place) + [place.core_partner(), place.pair_chip(), place.other_chip()])
     for copy in waits:
         copy.wait()
-    base = Gather(place, base_all, base_send, base_recv)
-    task = Gather(place, task_all, task_send, task_recv)
+
+    def base_piece(kind, index):
+        return base_all.at[kind, index]
+
+    def task_piece(kind, index):
+        return task_all.at[index, pl.ds(kind * 128, 128), :]
+
+    def task_partner(kind):
+        return task_own.at[1 - h, pl.ds(kind * 128, 128), :]
+
+    base = Gather(place, base_piece, lambda kind: base_piece(kind, place.dp), base_send, base_recv)
+    task = Gather(place, task_piece, task_partner, task_send, task_recv)
     rows = Rows(place, normed, rows_send, rows_recv)
     base.first()
 
@@ -444,7 +470,7 @@
             here = pl.multiple_of(chunk * CHUNK + at * 16, 16)
             wide = token_rows[pl.ds(here, 16), :].astype(F32)
             mean = jnp.mean(wide * wide, axis=-1, keepdims=True)
-            there = pl.multiple_of(place.mp * 128 + here, 16)
+            there = pl.multiple_of(rows.mine * 128 + here, 16)
             normed[pl.ds(there, 16), :] = (wide * lax.rsqrt(mean + 1e-06) * scale).astype(BF16)
             return carry
 
@@ -453,25 +479,28 @@
     for copy in later:
         copy.wait()
 
-    relays = list(range(128 // CHUNK))
+    chunks = list(range(128 // CHUNK))
     for at, (_, _, event) in enumerate(base.events()):
         event()
-        if at in (12, 18, 23):
-            rows.relay(relays.pop(0))
+        if at in (9, 16, 23):
+            rows.arrive(chunks.pop(0))
     task.first()
-    for chunk in relays:
+    for chunk in chunks:
+        rows.arrive(chunk)
+    for chunk in range(128 // CHUNK):
         rows.relay(chunk)
-    rows.rest()
+    rows.rest([rows.mine, rows.pair])
     ahead = [event for _, _, event in task.events()]
 
     def events(count):
         for _ in range(min(count, len(ahead))):
             ahead.pop(0)()
 
-    project(normed, base_all, bias, total)
-    events(4)
-    keys[...] = turn(total[:, :256], cosine[...], sine[...]).astype(BF16)
-    values[...] = total[:, 256:].astype(BF16)
+    mine, others = pl.multiple_of(h * 512, 512), pl.multiple_of(512 - h * 512, 512)
+    project(normed, mine, [base_all.at[0], base_all.at[1]], total)
+    events(6)
+    keys[...] = turn(total[:, :256] + bias[0:1, :], cosine[...], sine[...]).astype(BF16)
+    values[...] = (total[:, 256:] + bias[1:2, :]).astype(BF16)
     key_sum[...] = jnp.zeros_like(key_sum)
     value_sum[...] = jnp.zeros_like(value_sum)
     for quarter in range(4):
@@ -480,26 +509,30 @@
             base_head(quarter * 4 + at, query, cotangent, keys, values, key_sum, value_sum)
             return carry
 
-        lax.fori_loop(0, 4, base_step, 0)
-        events(4)
+        lax.fori_loop(0, 4, base_step, 0, unroll=4)
+        events(6)
 
     key_back = turn(key_sum[...], cosine[...], -sine[...]).astype(BF16)
     value_back = value_sum[...].astype(BF16)
-    back[:256, :] = key_back.astype(F32).T.astype(BF16)
-    back[256:, :] = value_back.astype(F32).T.astype(BF16)
+    back[0] = key_back.astype(F32).T.astype(BF16)
+    back[1] = value_back.astype(F32).T.astype(BF16)
+
+    def swap(source, target, at):
+        return pltpu.make_async_remote_copy(
+            src_ref=source,
+            dst_ref=target,
+            send_sem=pass_send.at[at],
+            recv_sem=pass_recv.at[at],
+            device_id=place.partner(),
+            device_id_type=MESH,
+        )
+
+    back_swap = swap(back.at[1 - h], back_kind.at[h], 0)
+    back_swap.start()
+    back_kind[h] = back[h]
     sums[0] = jnp.zeros_like(sums[0])
     sums[0, 0:1, :] = jnp.sum(key_back.astype(F32), axis=0, keepdims=True)
     sums[0, 1:2, :] = jnp.sum(value_back.astype(F32), axis=0, keepdims=True)
-    base.finish()
-
-    def grad_step(at, carry):
-        block = product(back[...], normed[:, pl.ds(pl.multiple_of(at * 256, 256), 256)]).astype(BF16)
-        base_all[0, at] = block[:256]
-        base_all[1, at] = block[256:]
-        return carry
-
-    lax.fori_loop(0, 32, grad_step, 0)
-    scatter = Scatter(place, base_all, land, part_send, part_recv)
 
     odd_y, odd_z = place.y % 2, place.z % 2
     mates = [
@@ -526,49 +559,88 @@
         if at + 1 < 5:
             mate_copy(at + 1).start()
 
+    mate_copy(0).start()
     events(len(ahead))
-    for kind in range(2):
-        scatter.first(kind)
-    for kind in range(2):
-        scatter.second_own(kind)
-    mate_copy(0).start()
-    project(normed, task_all, bias_task, total)
-    key_tangent[...] = turn(total[:, :256], cosine[...], sine[...]).astype(BF16)
-    value_tangent[...] = total[:, 256:].astype(BF16)
+
+    is_key = (h == 0).astype(F32)
+    kind_cosine = cosine[...] * is_key + (1.0 - is_key)
+    kind_sine = sine[...] * is_key
+    kind_bias = jnp.where(h == 0, bias_task[0:1, :], bias_task[1:2, :])
+    project(normed, mine, [task_all], task_total)
+    kv_tangent[h] = turn(task_total[...] + kind_bias, kind_cosine, kind_sine).astype(BF16)
+    for chunk in range(128 // CHUNK):
+        rows.arrive_far(chunk)
+    rows.rest([rows.other, rows.far])
+    project(normed, others, [task_all], task_total)
+    tangent_out[...] = turn(task_total[...] + kind_bias, kind_cosine, kind_sine).astype(BF16)
+    tangent_swap = swap(tangent_out, kv_tangent.at[h], 1)
+    tangent_swap.start()
+    back_swap.wait_recv()
+
+    scatter = Scatter(place, part, land, part_send, part_recv)
+
+    def gradients(count, offsets):
+        def step(at, carry):
+            off_y, off_z = offsets(at)
+            index = ((place.z + off_z) % 4) * 8 + ((place.y + off_y) % 4) * 2
+            pick = pl.ds(pl.multiple_of(index * 256, 512), 512)
+            block = product(back_kind[0], normed[:512, pick]) + product(back_kind[1], normed[512:, pick])
+            block = block.astype(BF16)
+            part[index] = block[:, :256]
+            part[index + 1] = block[:, 256:]
+            return carry
+
+        lax.fori_loop(0, count, step, 0)
+
+    gradients(4, lambda at: (2, at))
+    scatter.first(0)
+    gradients(3, lambda at: (3 + at, 2))
+    scatter.first(1)
+    gradients(6, lambda at: (1 + 2 * (at // 3), 3 + at % 3))
+    scatter.second_own(0)
+    gradients(3, lambda at: (0, 3 + at))
+    scatter.second_own(1)
+
+    def tangents(start, count):
+        def step(at, carry):
+            tangent_head(start + at, query, tangent, keys, kv_tangent.at[0], turned, context, context_tangent)
+            return carry
+
+        lax.fori_loop(0, count, step, 0, unroll=count)
+
+    mate_sum(0)
+    for across in (2, 1, 3, 0):
+        for kind in range(2):
+            scatter.second(kind, across)
+    mate_sum(1)
+    tangent_swap.wait_recv()
     for group in range(2):
         pick = slice(group * HEAD, (group + 1) * HEAD)
         turned[group, :HEAD, :] = values[:, pick].astype(F32).T.astype(BF16)
-        turned[group, HEAD:, :] = value_tangent[:, pick].astype(F32).T.astype(BF16)
-
-    def tangents(start, count):
-        def step(at, carry):
-            tangent_head(start + at, query, tangent, keys, key_tangent, turned, context, context_tangent)
-            return carry
-
-        lax.fori_loop(0, count, step, 0)
-
-    for at, across in enumerate((2, 1, 3, 0)):
-        mate_sum(at)
-        for kind in range(2):
-            scatter.second(kind, across)
-        if at % 2 == 1:
-            tangents(at // 2 * 4, 4)
-    mate_sum(4)
+        turned[group, HEAD:, :] = kv_tangent[1, :, pick].astype(F32).T.astype(BF16)
+    tangents(0, 4)
+    mate_sum(2)
     for across in (2, 1, 3, 0):
         for kind in range(2):
             scatter.third(kind, across)
-    tangents(8, 4)
+    tangents(4, 4)
+    mate_sum(3)
     for kind in range(2):
         scatter.fourth(kind)
+    tangents(8, 4)
+    mate_sum(4)
+    for kind in range(2):
+        scatter.fifth(kind, grad)
     tangents(12, 4)
-    for kind in range(2):
-        scatter.fifth(kind)
     for kind in range(2):
         scatter.last(kind, grad)
     bias_grad[...] = sums[5, 0:2, :]
     scatter.finish()
+    base.finish()
     task.finish()
     rows.finish()
+    back_swap.wait_send()
+    tangent_swap.wait_send()
 
 
 def layer(*operands):
@@ -579,19 +651,23 @@
         pltpu.VMEM((512, 2048), BF16),
         pltpu.VMEM((512, 2048), BF16),
         pltpu.VMEM((512, 2048), BF16),
-        pltpu.VMEM((512, 8192), BF16),
+        pltpu.VMEM((1024, 8192), BF16),
         pltpu.VMEM((2, 32, 256, 256), BF16),
-        pltpu.VMEM((2, 32, 256, 256), BF16),
-        pltpu.VMEM((2, 31, 256, 256), BF16),
+        pltpu.VMEM((2, 256, 256), BF16),
+        pltpu.VMEM((32, 256, 256), BF16),
+        pltpu.VMEM((32, 256, 256), BF16),
+        pltpu.VMEM((2, 31, 128, 256), BF16),
         pltpu.VMEM((512, 512), F32),
+        pltpu.VMEM((512, 256), F32),
         pltpu.VMEM((512, 256), BF16),
         pltpu.VMEM((512, 256), BF16),
-        pltpu.VMEM((512, 256), BF16),
+        pltpu.VMEM((2, 512, 256), BF16),
         pltpu.VMEM((512, 256), BF16),
         pltpu.VMEM((2, 256, 512), BF16),
         pltpu.VMEM((512, 256), F32),
         pltpu.VMEM((512, 256), F32),
-        pltpu.VMEM((512, 512), BF16),
+        pltpu.VMEM((2, 256, 512), BF16),
+        pltpu.VMEM((2, 256, 512), BF16),
         pltpu.VMEM((6, 8, 256), F32),
         pltpu.VMEM((5, 8, 256), F32),
         pltpu.SemaphoreType.DMA((8,)),
@@ -602,6 +678,8 @@
         pltpu.SemaphoreType.DMA((2, 31)),
         pltpu.SemaphoreType.DMA((5,)),
         pltpu.SemaphoreType.DMA((5,)),
+        pltpu.SemaphoreType.DMA((2,)),
+        pltpu.SemaphoreType.DMA((2,)),
     ]
     return pl.pallas_call(
         layer_kernel,

time: 189 us -> 156 us (0.83)
  Pallas kernels: 181 us -> 150 us
    pallas_call x1, Pallas kernels: 181 us -> 150 us  [layer(): pl.pallas_call(layer_kernel, out_shape=(jax.ShapeDtypeStruct((512, 2048),...]
where the time goes in v3:
time: 156 us
  Pallas kernels  150 us (96%)
  local copies, waits for them, and re-layouts  6.06 us (4%)
    pallas_call x1, Pallas kernels, layer(): pl.pallas_call(layer_kernel, out_shape=(jax.ShapeDtypeStruct((512, 2048),...  150 us
    unnamed x10, local copies, waits for them, and re-layouts  6.06 us

profile of v3, /device:TPU:0, one launch (start us, length us, event | category | flops | bytes accessed | tf_op | source)
XLA Modules:
  0.0 156.3 jit_solution(1735619911034259360)
XLA Ops:
  0.6 149.5 %layer.1 = (bf16[512,2048]{1,0:T(8,128)(2,1)}, bf16[512,2048]{1,0:T(8,128)(2,1)}, f32[2,256,256]{2,1,0:T(8,128)}, f32[2,256]{1,0:T(2,128)}) custom-call(bf16[128,8192]{1,0:T(8,128)(2,1)} %tokens.1, f32[1,8192]{1,0:T(1,128)} %bitcast.1, bf16[512,2048]{1,0:T(8,128)(2,1)} %query_in.1, bf16[512,2048]{1,0:T(8,128)(2,1)} %tangent_in.1, ...), custom_call_target="tpu_custom_call" | custom-call | tf_op jit(solution)/shard_map/layer/pallas_call | solution.py:684
  150.2 0.0 copy-start
  150.2 3.3 %copy.19 = bf16[512,2048]{1,0:T(8,128)(2,1)} copy(bf16[512,2048]{1,0:T(8,128)(2,1)} %get-tuple-element.8) | data formatting | bytes 4194304
  153.5 0.0 copy-done
  153.5 0.0 copy-start.1
  153.5 0.0 copy-start.2
  153.5 1.3 copy.20
  154.8 0.1 copy-done.1
  154.9 0.8 copy.21
  155.7 0.0 copy-done.2
  155.7 0.6 copy.22
Async XLA Ops:
  150.2 3.3 %copy-start = (bf16[512,2048]{1,0:T(8,128)(2,1)S(1)}, bf16[512,2048]{1,0:T(8,128)(2,1)}, u32[]{:S(2)}) copy-start(bf16[512,2048]{1,0:T(8,128)(2,1)} %get-tuple-element.9) | copy-start | bytes 6291460
  153.5 1.4 copy-start.1
  153.5 2.2 %copy-start.2 = (f32[2,256]{1,0:T(2,128)S(1)}, f32[2,256]{1,0:T(2,128)}, u32[]{:S(2)}) copy-start(f32[2,256]{1,0:T(2,128)} %get-tuple-element.11) | copy-start | bytes 6148

commit v4 on v3

--- a/solution.py
+++ b/solution.py
@@ -48,7 +48,10 @@
     barrier = pltpu.get_barrier_semaphore()
     for device in devices:
         pl.semaphore_signal(barrier, inc=1, device_id=device, device_id_type=MESH)
-    pl.semaphore_wait(barrier, len(devices))
+
+
+def greeted(devices):
+    pl.semaphore_wait(pltpu.get_barrier_semaphore(), len(devices))
 
 
 def ring_devices(place):
@@ -61,33 +64,47 @@
     ]
 
 
+def sent(amount, semaphore, place):
+    pltpu.make_async_remote_copy(
+        src_ref=amount,
+        dst_ref=amount,
+        send_sem=semaphore,
+        recv_sem=semaphore,
+        device_id=place.partner(),
+        device_id_type=MESH,
+    ).wait_send()
+
+
 class Gather:
-    def __init__(self, place, piece, partner_piece, send, recv):
-        self.place, self.piece, self.partner_piece = place, piece, partner_piece
+    def __init__(self, place, piece, partner_piece, sent, send, recv):
+        self.place, self.piece, self.partner_piece, self.sent = place, piece, partner_piece, sent
         self.send, self.recv = send, recv
-        self.slots = [0, 0]
-        self.started = []
-
-    def copy(self, kind, index, device, slot, source=None):
+
+    def copy(self, kind, index, device, source=None):
         block = self.piece(kind, index)
         return pltpu.make_async_remote_copy(
             src_ref=block if source is None else source,
             dst_ref=block,
-            send_sem=self.send.at[kind, slot],
-            recv_sem=self.recv.at[kind, index],
+            send_sem=self.send.at[kind],
+            recv_sem=self.recv.at[kind, index // 2],
             device_id=device,
             device_id_type=MESH,
         )
 
     def start(self, kind, index, device, source=None):
-        slot = self.slots[kind]
-        self.slots[kind] += 1
-        copy = self.copy(kind, index, device, slot, source)
-        copy.start()
-        self.started.append(copy)
-
-    def wait(self, kind, index):
-        self.copy(kind, index, self.place.partner(), 0).wait_recv()
+        self.copy(kind, index, device, source).start()
+
+    def wait(self, kind, along, across):
+        index = self.place.index(kind, along, across, 0)
+        amount = self.sent(kind, 2)
+        pltpu.make_async_remote_copy(
+            src_ref=amount,
+            dst_ref=amount,
+            send_sem=self.send.at[kind],
+            recv_sem=self.recv.at[kind, index // 2],
+            device_id=self.place.partner(),
+            device_id_type=MESH,
+        ).wait_recv()
 
     def spread(self, kind, index, along):
         if along:
@@ -96,11 +113,13 @@
         self.start(kind, index, self.place.device(kind, 0, 1))
         self.start(kind, index, self.place.device(kind, 0, -1))
 
+    def swap(self):
+        for kind in range(2):
+            self.start(kind, self.place.dp, self.place.partner(), self.partner_piece(kind))
+
     def first(self):
         own = self.place.dp
         for kind in range(2):
-            self.start(kind, own, self.place.partner(), self.partner_piece(kind))
-        for kind in range(2):
             self.spread(kind, own, True)
 
     def events(self):
@@ -108,35 +127,30 @@
 
         def partner(kind):
             other = place.index(kind, 0, 0, 1 - place.h)
-            self.wait(kind, other)
+            self.copy(kind, other, place.partner()).wait_recv()
             self.spread(kind, other, True)
 
-        def side(kind, along):
-            near, far = (0, 1) if along < 0 else (1, 0)
-            index = place.index(kind, along, 0, near)
-            self.wait(kind, index)
-            self.start(kind, index, place.device(kind, -along, 0))
-            self.spread(kind, index, False)
-            index = place.index(kind, along, 0, far)
-            self.wait(kind, index)
-            self.spread(kind, index, False)
+        def side_relay(kind, along):
+            self.wait(kind, along, 0)
+            near = 0 if along < 0 else 1
+            self.start(kind, place.index(kind, along, 0, near), place.device(kind, -along, 0))
+
+        def side_spread(kind, along):
+            for half in range(2):
+                self.spread(kind, place.index(kind, along, 0, half), False)
 
         def opposite(kind):
+            self.wait(kind, 2, 0)
             for half in range(2):
-                index = place.index(kind, 2, 0, half)
-                self.wait(kind, index)
-                self.spread(kind, index, False)
+                self.spread(kind, place.index(kind, 2, 0, half), False)
 
         def across(kind, along, step):
-            near, far = (0, 1) if step < 0 else (1, 0)
-            index = place.index(kind, along, step, near)
-            self.wait(kind, index)
-            self.start(kind, index, place.device(kind, 0, -step))
-            self.wait(kind, place.index(kind, along, step, far))
+            self.wait(kind, along, step)
+            near = 0 if step < 0 else 1
+            self.start(kind, place.index(kind, along, step, near), place.device(kind, 0, -step))
 
         def across_opposite(kind, along):
-            for half in range(2):
-                self.wait(kind, place.index(kind, along, 2, half))
+            self.wait(kind, along, 2)
 
         result = []
 
@@ -145,8 +159,10 @@
                 result.append((kind, blocks, functools.partial(function, kind, *rest)))
 
         add([(0, 0)], partner)
-        add([(-1, 0)], side, -1)
-        add([(1, 0)], side, 1)
+        add([(-1, 0)], side_relay, -1)
+        add([(1, 0)], side_relay, 1)
+        add([], side_spread, -1)
+        add([], side_spread, 1)
         add([(0, -1)], across, 0, -1)
         add([(0, 1)], across, 0, 1)
         add([(2, 0)], opposite)
@@ -159,12 +175,13 @@
         return result
 
     def finish(self):
-        for copy in self.started:
-            copy.wait_send()
-
-
-GATHER_SEMS = [pltpu.SemaphoreType.DMA((2, 31)), pltpu.SemaphoreType.DMA((2, 32))]
-CHUNK = 32
+        for kind in range(2):
+            sent(self.sent(kind, 31), self.send.at[kind], self.place)
+
+
+GATHER_SEMS = [pltpu.SemaphoreType.DMA((2,)), pltpu.SemaphoreType.DMA((2, 16))]
+CHUNKS = 8
+CHUNK = 8192 // CHUNKS
 
 
 class Rows:
@@ -176,24 +193,21 @@
         self.other = place.other_block()
         x = (h * 2 + mp // 2 + 2) % 4
         self.far = x * 2 + mp % 2
-        self.started = []
 
     def copy(self, owner, chunk, device, lane):
-        rows = pl.multiple_of(owner * 128 + chunk * CHUNK, CHUNK)
-        block = self.whole.at[pl.ds(rows, CHUNK), :]
+        rows = pl.ds(pl.multiple_of(owner * 128, 128), 128)
+        block = self.whole.at[rows, pl.ds(chunk * CHUNK, CHUNK)]
         return pltpu.make_async_remote_copy(
             src_ref=block,
             dst_ref=block,
-            send_sem=self.send.at[lane, chunk],
+            send_sem=self.send.at[lane],
             recv_sem=self.recv.at[owner, chunk],
             device_id=device,
             device_id_type=MESH,
         )
 
     def start(self, owner, chunk, device, lane):
-        copy = self.copy(owner, chunk, device, lane)
-        copy.start()
-        self.started.append(copy)
+        self.copy(owner, chunk, device, lane).start()
 
     def own(self, chunk):
         self.start(self.mine, chunk, self.place.pair_chip(), 0)
@@ -203,13 +217,16 @@
     def wait(self, owner, chunk):
         self.copy(owner, chunk, self.place.core_partner(), 0).wait_recv()
 
-    def arrive(self, chunk):
-        for owner, lane in ((self.pair, 3), (self.other, 4)):
-            self.wait(owner, chunk)
-            self.start(owner, chunk, self.place.core_partner(), lane)
+    def arrive_pair(self, chunk):
+        self.wait(self.pair, chunk)
+        self.start(self.pair, chunk, self.place.core_partner(), 3)
+
+    def arrive_other(self, chunk):
+        self.wait(self.other, chunk)
+        self.start(self.other, chunk, self.place.core_partner(), 4)
 
     def relay(self, chunk):
-        if chunk < 128 // CHUNK // 2:
+        if chunk < CHUNKS // 2:
             self.start(self.pair, chunk, self.place.other_chip(), 5)
         else:
             self.start(self.other, chunk, self.place.pair_chip(), 5)
@@ -218,52 +235,57 @@
         self.wait(self.far, chunk)
         self.start(self.far, chunk, self.place.core_partner(), 6)
 
-    def rest(self, owners):
+    def rest(self, owners, chunk):
         for owner in owners:
-            for chunk in range(128 // CHUNK):
-                self.wait(owner + 1 - 2 * (owner % 2), chunk)
+            self.wait(owner + 1 - 2 * (owner % 2), chunk)
 
     def finish(self):
-        for copy in self.started:
-            copy.wait_send()
-
-
-ROWS_SEMS = [pltpu.SemaphoreType.DMA((7, 128 // CHUNK)), pltpu.SemaphoreType.DMA((8, 128 // CHUNK))]
+        for lane in range(7):
+            sent(self.whole.at[pl.ds(0, 128), :], self.send.at[lane], self.place)
+
+
+ROWS_SEMS = [pltpu.SemaphoreType.DMA((7,)), pltpu.SemaphoreType.DMA((8, CHUNKS))]
 
 
 class Scatter:
     def __init__(self, place, part, land, send, recv):
         self.place, self.part, self.land, self.send, self.recv = place, part, land, send, recv
-        self.slots = [0, 0]
-        self.started = []
 
     def own(self, kind, along, across, half):
         return self.part.at[self.place.index(kind, along, across, half), pl.ds(kind * 128, 128), :]
 
-    def copy(self, kind, block, spot, device, slot):
+    def copy(self, kind, block, spot, device):
         return pltpu.make_async_remote_copy(
             src_ref=block,
             dst_ref=self.land.at[kind, spot],
-            send_sem=self.send.at[kind, slot],
-            recv_sem=self.recv.at[kind, spot],
+            send_sem=self.send.at[kind],
+            recv_sem=self.recv.at[kind, self.lane(spot)],
             device_id=device,
             device_id_type=MESH,
         )
 
+    @staticmethod
+    def lane(spot):
+        if 16 <= spot < 24:
+            return spot - 8
+        return spot - 2 if spot in (28, 29) else spot
+
     def start(self, kind, block, spot, device):
-        slot = self.slots[kind]
-        self.slots[kind] += 1
-        copy = self.copy(kind, block, spot, device, slot)
-        copy.start()
-        self.started.append(copy)
-
-    def wait(self, kind, spot):
-        block = self.land.at[kind, spot]
-        self.copy(kind, block, spot, self.place.partner(), 0).wait_recv()
+        self.copy(kind, block, spot, device).start()
+
+    def wait(self, kind, spots):
+        amount = self.land.at[kind, pl.ds(0, len(spots))]
+        pltpu.make_async_remote_copy(
+            src_ref=amount,
+            dst_ref=amount,
+            send_sem=self.send.at[kind],
+            recv_sem=self.recv.at[kind, self.lane(spots[0])],
+            device_id=self.place.partner(),
+            device_id_type=MESH,
+        ).wait_recv()
 
     def add(self, kind, block, spots):
-        for spot in spots:
-            self.wait(kind, spot)
+        self.wait(kind, spots)
 
         def step(at, carry):
             rows = pl.ds(pl.multiple_of(at * 64, 64), 64)
@@ -281,13 +303,12 @@
                 block = self.own(kind, 2, across, half)
                 self.start(kind, block, half * 4 + across, self.place.device(kind, along, 0))
 
-    def second_own(self, kind):
-        for across in (2, 1, 3, 0):
-            for side, along in ((0, 1), (1, -1)):
-                half = 1 - side
-                block = self.own(kind, along, across, half)
-                spot = 8 + side * 8 + across * 2 + half
-                self.start(kind, block, spot, self.place.device(kind, along, 0))
+    def second_own(self, kind, across):
+        for side, along in ((0, 1), (1, -1)):
+            half = 1 - side
+            block = self.own(kind, along, across, half)
+            spot = 8 + side * 8 + across * 2 + half
+            self.start(kind, block, spot, self.place.device(kind, along, 0))
 
     def second(self, kind, across):
         for side, along in ((0, 1), (1, -1)):
@@ -319,12 +340,22 @@
 
     def fifth(self, kind, grad):
         for half in (1 - self.place.h, self.place.h):
-            for side in range(2):
-                self.wait(kind, 26 + side * 2 + half)
+            self.wait_last(kind, half)
         block = self.own(kind, 0, 0, 1 - self.place.h)
         block[...] = self.summed(kind, 1 - self.place.h).astype(jnp.bfloat16)
         self.start(kind, block, 30, self.place.partner())
         grad[self.place.h, :, kind * 128 : (kind + 1) * 128] = self.summed(kind, self.place.h).T
+
+    def wait_last(self, kind, half):
+        amount = self.land.at[kind, pl.ds(0, 2)]
+        pltpu.make_async_remote_copy(
+            src_ref=amount,
+            dst_ref=amount,
+            send_sem=self.send.at[kind],
+            recv_sem=self.recv.at[kind, 26 + half],
+            device_id=self.place.partner(),
+            device_id_type=MESH,
+        ).wait_recv()
 
     def summed(self, kind, half):
         total = self.own(kind, 0, 0, half)[...].astype(jnp.float32)
@@ -333,13 +364,13 @@
         return total
 
     def last(self, kind, grad):
-        self.wait(kind, 30)
+        self.wait(kind, [30])
         block = self.land[kind, 30].astype(jnp.float32)
         grad[1 - self.place.h, :, kind * 128 : (kind + 1) * 128] = block.T
 
     def finish(self):
-        for copy in self.started:
-            copy.wait_send()
+        for kind in range(2):
+            sent(self.land.at[kind], self.send.at[kind], self.place)
 
 
 FACTOR = HEAD ** (-0.5)
@@ -408,9 +439,7 @@
         context_tangent[rows, columns(head)] = (first[HEAD:] + second).T.astype(BF16)
 
 
-def project(normed, start, weights, total):
-    total[...] = jnp.zeros_like(total)
-
+def project(normed, start, weights, total, first, last):
     def step(at, carry):
         for kind, weight in enumerate(weights):
             sums = 0.0
@@ -421,15 +450,15 @@
             total[:, kind * 256 : (kind + 1) * 256] += sums
         return carry
 
-    lax.fori_loop(0, 8, step, 0)
+    lax.fori_loop(first, last, step, 0)
 
 
 def layer_kernel(
     tokens, gain, query_in, tangent_in, kv_in, bias, task_in, bias_task, cotangent_in, cosine, sine,
-    context, context_tangent, grad, bias_grad,
-    token_rows, query, tangent, cotangent, normed, base_all, task_own, task_all, part, land, total, task_total,
+    context_out, context_tangent_out, grad, bias_grad,
+    context, context_tangent, token_rows, query, tangent, cotangent, normed, base_all, task_own, task_all, part, land, total, task_total,
     keys, values, kv_tangent, tangent_out, turned, key_sum, value_sum, back, back_kind, sums, sums_land,
-    local, base_send, base_recv, task_send, task_recv, rows_send, rows_recv,
+    local, out_sems, base_send, base_recv, task_send, task_recv, rows_send, rows_recv,
     part_send, part_recv, sums_send, sums_recv, pass_send, pass_recv,
 ):
     place = Place()
@@ -443,74 +472,102 @@
     waits = [load(kv_in.at[kind], base_all.at[kind, place.dp], kind) for kind in range(2)]
     waits.append(load(task_in, task_own, 2))
     waits.append(load(task_in.at[h], task_all.at[place.dp], 3))
-    waits.append(load(tokens, token_rows, 4))
+    load_tokens = load(tokens, token_rows, 4)
     later = [load(query_in, query, 5), load(cotangent_in, cotangent, 6), load(tangent_in, tangent, 7)]
-    greet(ring_devices(place) + [place.core_partner(), place.pair_chip(), place.other_chip()])
+    around = ring_devices(place) + [place.core_partner(), place.pair_chip(), place.other_chip()]
+    greet(around)
+
+    def base_piece(kind, index):
+        return base_all.at[kind, index]
+
+    def task_piece(kind, index):
+        return task_all.at[index, pl.ds(kind * 128, 128), :]
+
+    def task_partner(kind):
+        return task_own.at[1 - h, pl.ds(kind * 128, 128), :]
+
+    base = Gather(
+        place, base_piece, lambda kind: base_piece(kind, place.dp),
+        lambda kind, count: base_all.at[kind, pl.ds(0, count)], base_send, base_recv,
+    )
+    task = Gather(
+        place, task_piece, task_partner,
+        lambda kind, count: task_all.at[pl.ds(0, count), pl.ds(0, 128), :], task_send, task_recv,
+    )
+    rows = Rows(place, normed, rows_send, rows_recv)
     for copy in waits:
         copy.wait()
-
-    def base_piece(kind, index):
-        return base_all.at[kind, index]
-
-    def task_piece(kind, index):
-        return task_all.at[index, pl.ds(kind * 128, 128), :]
-
-    def task_partner(kind):
-        return task_own.at[1 - h, pl.ds(kind * 128, 128), :]
-
-    base = Gather(place, base_piece, lambda kind: base_piece(kind, place.dp), base_send, base_recv)
-    task = Gather(place, task_piece, task_partner, task_send, task_recv)
-    rows = Rows(place, normed, rows_send, rows_recv)
+    greeted(around)
+    base.swap()
+    task.swap()
     base.first()
-
+    load_tokens.wait()
     scale = gain[...]
-    for chunk in range(128 // CHUNK):
-
-        def norm(at, carry, chunk=chunk):
-            here = pl.multiple_of(chunk * CHUNK + at * 16, 16)
-            wide = token_rows[pl.ds(here, 16), :].astype(F32)
-            mean = jnp.mean(wide * wide, axis=-1, keepdims=True)
-            there = pl.multiple_of(rows.mine * 128 + here, 16)
-            normed[pl.ds(there, 16), :] = (wide * lax.rsqrt(mean + 1e-06) * scale).astype(BF16)
-            return carry
-
-        lax.fori_loop(0, CHUNK // 16, norm, 0)
+
+    def norm(at, carry):
+        here = pl.multiple_of(at * 16, 16)
+        wide = token_rows[pl.ds(here, 16), :].astype(F32)
+        mean = jnp.mean(wide * wide, axis=-1, keepdims=True)
+        there = pl.multiple_of(rows.mine * 128 + here, 16)
+        normed[pl.ds(there, 16), :] = (wide * lax.rsqrt(mean + 1e-06) * scale).astype(BF16)
+        return carry
+
+    lax.fori_loop(0, 8, norm, 0)
+    for chunk in range(CHUNKS):
         rows.own(chunk)
     for copy in later:
         copy.wait()
 
-    chunks = list(range(128 // CHUNK))
     for at, (_, _, event) in enumerate(base.events()):
         event()
-        if at in (9, 16, 23):
-            rows.arrive(chunks.pop(0))
+        if at in (16, 19, 22, 26, 31):
+            chunk = (16, 19, 22, 26, 31).index(at)
+            rows.arrive_pair(chunk)
+            if chunk > 0:
+                rows.arrive_other(chunk - 1)
     task.first()
-    for chunk in chunks:
-        rows.arrive(chunk)
-    for chunk in range(128 // CHUNK):
-        rows.relay(chunk)
-    rows.rest([rows.mine, rows.pair])
     ahead = [event for _, _, event in task.events()]
 
     def events(count):
         for _ in range(min(count, len(ahead))):
             ahead.pop(0)()
 
+    events(2)
     mine, others = pl.multiple_of(h * 512, 512), pl.multiple_of(512 - h * 512, 512)
-    project(normed, mine, [base_all.at[0], base_all.at[1]], total)
-    events(6)
+    total[...] = jnp.zeros_like(total)
+    both = [base_all.at[0], base_all.at[1]]
+    rows.arrive_pair(5)
+    for chunk in range(4):
+        rows.rest([rows.mine, rows.pair], chunk)
+    project(normed, mine, both, total, 0, 4)
+    for chunk in (4, 5, 6, 7):
+        if chunk >= 6:
+            rows.arrive_pair(chunk)
+        if chunk == 7:
+            for other in range(CHUNKS // 2):
+                rows.relay(other)
+            for other in range(4, 7):
+                rows.arrive_other(other)
+                rows.relay(other)
+        rows.rest([rows.mine, rows.pair], chunk)
+        project(normed, mine, both, total, chunk, chunk + 1)
+    rows.arrive_other(7)
+    rows.relay(7)
     keys[...] = turn(total[:, :256] + bias[0:1, :], cosine[...], sine[...]).astype(BF16)
     values[...] = (total[:, 256:] + bias[1:2, :]).astype(BF16)
+    events(8)
     key_sum[...] = jnp.zeros_like(key_sum)
     value_sum[...] = jnp.zeros_like(value_sum)
-    for quarter in range(4):
-
-        def base_step(at, carry, quarter=quarter):
-            base_head(quarter * 4 + at, query, cotangent, keys, values, key_sum, value_sum)
+    for part_of in range(8):
+
+        def base_step(at, carry, part_of=part_of):
+            base_head(part_of * 2 + at, query, cotangent, keys, values, key_sum, value_sum)
             return carry
 
-        lax.fori_loop(0, 4, base_step, 0, unroll=4)
-        events(6)
+        lax.fori_loop(0, 2, base_step, 0, unroll=2)
+        events((4, 0, 2, 4, 2, 4, 4, 4)[part_of])
+        for chunk in ((), (), (), (), (), (0, 4), (), (1, 5))[part_of]:
+            rows.arrive_far(chunk)
 
     key_back = turn(key_sum[...], cosine[...], -sine[...]).astype(BF16)
     value_back = value_sum[...].astype(BF16)
@@ -566,15 +623,27 @@
     kind_cosine = cosine[...] * is_key + (1.0 - is_key)
     kind_sine = sine[...] * is_key
     kind_bias = jnp.where(h == 0, bias_task[0:1, :], bias_task[1:2, :])
-    project(normed, mine, [task_all], task_total)
+    task_total[...] = jnp.zeros_like(task_total)
+    project(normed, mine, [task_all], task_total, 0, 8)
     kv_tangent[h] = turn(task_total[...] + kind_bias, kind_cosine, kind_sine).astype(BF16)
-    for chunk in range(128 // CHUNK):
+    task_total[...] = jnp.zeros_like(task_total)
+
+    def project_others(chunks):
+        for chunk in chunks:
+            rows.rest([rows.other, rows.far], chunk)
+            project(normed, others, [task_all], task_total, chunk, chunk + 1)
+
+    mate_sum(0)
+    for chunk in (2, 6):
         rows.arrive_far(chunk)
-    rows.rest([rows.other, rows.far])
-    project(normed, others, [task_all], task_total)
-    tangent_out[...] = turn(task_total[...] + kind_bias, kind_cosine, kind_sine).astype(BF16)
-    tangent_swap = swap(tangent_out, kv_tangent.at[h], 1)
-    tangent_swap.start()
+    project_others((0, 1, 4, 5))
+    mate_sum(1)
+    for chunk in (3, 7):
+        rows.arrive_far(chunk)
+    project_others((2, 6))
+    mate_sum(2)
+    for chunk in (3, 7):
+        rows.rest([rows.other, rows.far], chunk)
     back_swap.wait_recv()
 
     scatter = Scatter(place, part, land, part_send, part_recv)
@@ -596,10 +665,16 @@
     scatter.first(0)
     gradients(3, lambda at: (3 + at, 2))
     scatter.first(1)
+    mate_sum(3)
+    for chunk in (3, 7):
+        project(normed, others, [task_all], task_total, chunk, chunk + 1)
+    tangent_out[...] = turn(task_total[...] + kind_bias, kind_cosine, kind_sine).astype(BF16)
+    tangent_swap = swap(tangent_out, kv_tangent.at[h], 1)
+    tangent_swap.start()
     gradients(6, lambda at: (1 + 2 * (at // 3), 3 + at % 3))
-    scatter.second_own(0)
     gradients(3, lambda at: (0, 3 + at))
-    scatter.second_own(1)
+
+    outs = []
 
     def tangents(start, count):
         def step(at, carry):
@@ -607,34 +682,43 @@
             return carry
 
         lax.fori_loop(0, count, step, 0, unroll=count)
-
-    mate_sum(0)
+        pick = pl.ds(start * HEAD, count * HEAD)
+        for source, target in ((context, context_out), (context_tangent, context_tangent_out)):
+            outs.append(pltpu.make_async_copy(source.at[:, pick], target.at[:, pick], out_sems.at[len(outs)]))
+            outs[-1].start()
+
     for across in (2, 1, 3, 0):
         for kind in range(2):
+            scatter.second_own(kind, across)
+        for kind in range(2):
             scatter.second(kind, across)
-    mate_sum(1)
     tangent_swap.wait_recv()
     for group in range(2):
         pick = slice(group * HEAD, (group + 1) * HEAD)
         turned[group, :HEAD, :] = values[:, pick].astype(F32).T.astype(BF16)
         turned[group, HEAD:, :] = kv_tangent[1, :, pick].astype(F32).T.astype(BF16)
-    tangents(0, 4)
-    mate_sum(2)
-    for across in (2, 1, 3, 0):
+    def third(across):
         for kind in range(2):
             scatter.third(kind, across)
+
+    tangents(0, 4)
+    third(2)
     tangents(4, 4)
-    mate_sum(3)
+    third(1)
+    third(3)
+    tangents(8, 4)
     for kind in range(2):
         scatter.fourth(kind)
-    tangents(8, 4)
-    mate_sum(4)
+    third(0)
     for kind in range(2):
         scatter.fifth(kind, grad)
     tangents(12, 4)
+    mate_sum(4)
+    bias_grad[...] = sums[5, 0:2, :]
     for kind in range(2):
         scatter.last(kind, grad)
-    bias_grad[...] = sums[5, 0:2, :]
+    for copy in outs:
+        copy.wait()
     scatter.finish()
     base.finish()
     task.finish()
@@ -647,6 +731,8 @@
     vmem = pl.BlockSpec(memory_space=pltpu.VMEM)
     hbm = pl.BlockSpec(memory_space=pl.ANY)
     scratch = [
+        pltpu.VMEM((512, 2048), BF16),
+        pltpu.VMEM((512, 2048), BF16),
         pltpu.VMEM((128, 8192), BF16),
         pltpu.VMEM((512, 2048), BF16),
         pltpu.VMEM((512, 2048), BF16),
@@ -671,10 +757,11 @@
         pltpu.VMEM((6, 8, 256), F32),
         pltpu.VMEM((5, 8, 256), F32),
         pltpu.SemaphoreType.DMA((8,)),
+        pltpu.SemaphoreType.DMA((8,)),
         *GATHER_SEMS,
         *GATHER_SEMS,
         *ROWS_SEMS,
-        pltpu.SemaphoreType.DMA((2, 31)),
+        pltpu.SemaphoreType.DMA((2,)),
         pltpu.SemaphoreType.DMA((2, 31)),
         pltpu.SemaphoreType.DMA((5,)),
         pltpu.SemaphoreType.DMA((5,)),
@@ -690,13 +777,47 @@
             jax.ShapeDtypeStruct((2, 256), F32),
         ),
         in_specs=[hbm, vmem, hbm, hbm, hbm, vmem, hbm, vmem, hbm, vmem, vmem],
-        out_specs=(vmem,) * 4,
+        out_specs=(hbm, hbm, vmem, vmem),
         scratch_shapes=scratch,
         compiler_params=pltpu.CompilerParams(
             collective_id=0, has_side_effects=True, vmem_limit_bytes=62 * 1024 * 1024
         ),
         name="layer",
     )(*operands)
+
+
+def hand_over_kernel(context, context_tangent, grad, bias_grad, *rest):
+    outs, held, loads, stores = rest[:4], rest[4:8], rest[8], rest[9]
+    pieces = []
+    for at in range(4):
+        rows = pl.ds(at * 128, 128)
+        for which, source in ((0, context), (1, context_tangent)):
+            pieces.append((source.at[rows, :], held[which].at[rows, :], outs[which].at[rows, :]))
+    pieces.append((grad, held[2], outs[2]))
+    pieces.append((bias_grad, held[3], outs[3]))
+    arriving = [pltpu.make_async_copy(a, b, loads.at[at]) for at, (a, b, _) in enumerate(pieces)]
+    leaving = [pltpu.make_async_copy(b, c, stores.at[at]) for at, (_, b, c) in enumerate(pieces)]
+    for copy in arriving:
+        copy.start()
+    for copy, after in zip(arriving, leaving):
+        copy.wait()
+        after.start()
+    for copy in leaving:
+        copy.wait()
+
+
+def hand_over(*results):
+    hbm = pl.BlockSpec(memory_space=pl.ANY)
+    return pl.pallas_call(
+        hand_over_kernel,
+        out_shape=tuple(jax.ShapeDtypeStruct(one.shape, one.dtype) for one in results),
+        in_specs=[hbm] * 4,
+        out_specs=(hbm,) * 4,
+        scratch_shapes=[pltpu.VMEM(one.shape, one.dtype) for one in results]
+        + [pltpu.SemaphoreType.DMA((10,)), pltpu.SemaphoreType.DMA((10,))],
+        compiler_params=pltpu.CompilerParams(vmem_limit_bytes=62 * 1024 * 1024),
+        name="hand_over",
+    )(*results)
 
 
 def turning_tables():
@@ -712,10 +833,10 @@
 
 def body(tokens, gain, query, query_tangent, kv_weight, kv_bias, kv_task, kv_bias_task, cotangent):
     cosine, sine = turning_tables()
-    return layer(
+    return hand_over(*layer(
         tokens, gain.reshape(1, -1), query, query_tangent, kv_weight, kv_bias, kv_task, kv_bias_task, cotangent,
         jnp.asarray(cosine), jnp.asarray(sine),
-    )
+    ))
 
 
 def solution(mesh):

time: 156 us -> 135 us (0.87)
  Pallas kernels: 150 us -> 134 us
  local copies, waits for them, and re-layouts: 6.06 us -> 0 us
    pallas_call x1, Pallas kernels: 150 us -> 130 us  [layer(): pl.pallas_call(layer_kernel, out_shape=(jax.ShapeDtypeStruct((512, 2048),...]
    unnamed x10 -> x0, local copies, waits for them, and re-layouts: 6.06 us -> none
    pallas_call x0 -> x1, Pallas kernels: none -> 4.18 us  [hand_over(): pl.pallas_call(hand_over_kernel, out_shape=tuple((jax.ShapeDtypeStruct(on...]
where the time goes in v4:
time: 135 us
  Pallas kernels  134 us (99%)
    pallas_call x1, Pallas kernels, layer(): pl.pallas_call(layer_kernel, out_shape=(jax.ShapeDtypeStruct((512, 2048),...  130 us
    pallas_call x1, Pallas kernels, hand_over(): pl.pallas_call(hand_over_kernel, out_shape=tuple((jax.ShapeDtypeStruct(on...  4.18 us

profile of v4, /device:TPU:0, one launch (start us, length us, event | category | flops | bytes accessed | tf_op | source)
XLA Modules:
  0.0 134.9 jit_solution(4059194140538568088)
XLA Ops:
  0.6 129.9 %layer.1 = (bf16[512,2048]{1,0:T(8,128)(2,1)}, bf16[512,2048]{1,0:T(8,128)(2,1)}, f32[2,256,256]{2,1,0:T(8,128)}, f32[2,256]{1,0:T(2,128)}) custom-call(bf16[128,8192]{1,0:T(8,128)(2,1)} %tokens.1, f32[1,8192]{1,0:T(1,128)} %bitcast.1, bf16[512,2048]{1,0:T(8,128)(2,1)} %query_in.1, bf16[512,2048]{1,0:T(8,128)(2,1)} %tangent_in.1, ...), custom_call_target="tpu_custom_call" | custom-call | tf_op jit(solution)/shard_map/layer/pallas_call | solution.py:771
  130.6 4.2 %hand_over.1 = (bf16[512,2048]{1,0:T(8,128)(2,1)}, bf16[512,2048]{1,0:T(8,128)(2,1)}, f32[2,256,256]{2,1,0:T(8,128)}, f32[2,256]{1,0:T(2,128)}) custom-call(bf16[512,2048]{1,0:T(8,128)(2,1)} %get-tuple-element.8.context, bf16[512,2048]{1,0:T(8,128)(2,1)} %get-tuple-element.9.context_tangent, f32[2,256,256]{2,1,0:T(8,128)} %get-tuple-element.10.grad, ...), custom_call_target="tpu_custom_call" | custom-call | tf_op jit(solution)/shard_map/hand_over/pallas_call | solution.py:811

commit v5 on v4

--- a/solution.py
+++ b/solution.py
@@ -127,7 +127,8 @@
 
         def partner(kind):
             other = place.index(kind, 0, 0, 1 - place.h)
-            self.copy(kind, other, place.partner()).wait_recv()
+            if self.partner_piece is not None:
+                self.copy(kind, other, place.partner()).wait_recv()
             self.spread(kind, other, True)
 
         def side_relay(kind, along):
@@ -176,7 +177,7 @@
 
     def finish(self):
         for kind in range(2):
-            sent(self.sent(kind, 31), self.send.at[kind], self.place)
+            sent(self.sent(kind, 31 if self.partner_piece else 30), self.send.at[kind], self.place)
 
 
 GATHER_SEMS = [pltpu.SemaphoreType.DMA((2,)), pltpu.SemaphoreType.DMA((2, 16))]
@@ -185,63 +186,69 @@
 
 
 class Rows:
-    def __init__(self, place, whole, send, recv):
-        self.place, self.whole, self.send, self.recv = place, whole, send, recv
-        mp, h = place.mp, place.h
-        self.mine = h * 4 + mp
-        self.pair = h * 4 + (mp + 2) % 4
-        self.other = place.other_block()
-        x = (h * 2 + mp // 2 + 2) % 4
-        self.far = x * 2 + mp % 2
+    def __init__(self, place, whole, others, send, recv):
+        self.place, self.whole, self.others, self.send, self.recv = place, whole, others, send, recv
+        self.mine, self.pair = place.mp, (place.mp + 2) % 4
+        self.other = place.other_block() % 4
+        self.far = (self.other + 2) % 4
 
     def copy(self, owner, chunk, device, lane):
         rows = pl.ds(pl.multiple_of(owner * 128, 128), 128)
         block = self.whole.at[rows, pl.ds(chunk * CHUNK, CHUNK)]
+        return self.move(block, block, self.recv.at[owner, chunk], device, lane)
+
+    def move(self, source, target, semaphore, device, lane):
         return pltpu.make_async_remote_copy(
-            src_ref=block,
-            dst_ref=block,
+            src_ref=source,
+            dst_ref=target,
             send_sem=self.send.at[lane],
-            recv_sem=self.recv.at[owner, chunk],
+            recv_sem=semaphore,
             device_id=device,
             device_id_type=MESH,
         )
 
-    def start(self, owner, chunk, device, lane):
-        self.copy(owner, chunk, device, lane).start()
+    def across(self, owner, chunk, device, lane, forward):
+        rows = pl.ds(pl.multiple_of(owner * 128, 128), 128)
+        for at in range(2):
+            block = self.others.at[chunk * 2 + at, rows, :]
+            source = block
+            if not forward:
+                first = pl.multiple_of((chunk * 2 + at) * 512 + (1 - self.place.h) * 256, 256)
+                source = self.whole.at[rows, pl.ds(first, 256)]
+            self.move(source, block, self.recv.at[4 + owner, chunk], device, lane).start()
 
     def own(self, chunk):
-        self.start(self.mine, chunk, self.place.pair_chip(), 0)
-        self.start(self.mine, chunk, self.place.other_chip(), 1)
-        self.start(self.mine, chunk, self.place.core_partner(), 2)
-
-    def wait(self, owner, chunk):
-        self.copy(owner, chunk, self.place.core_partner(), 0).wait_recv()
+        self.copy(self.mine, chunk, self.place.pair_chip(), 0).start()
+        self.copy(self.mine, chunk, self.place.core_partner(), 1).start()
+        self.across(self.mine, chunk, self.place.other_chip(), 2, False)
 
     def arrive_pair(self, chunk):
-        self.wait(self.pair, chunk)
-        self.start(self.pair, chunk, self.place.core_partner(), 3)
-
-    def arrive_other(self, chunk):
-        self.wait(self.other, chunk)
-        self.start(self.other, chunk, self.place.core_partner(), 4)
-
-    def relay(self, chunk):
-        if chunk < CHUNKS // 2:
-            self.start(self.pair, chunk, self.place.other_chip(), 5)
-        else:
-            self.start(self.other, chunk, self.place.pair_chip(), 5)
-
-    def arrive_far(self, chunk):
-        self.wait(self.far, chunk)
-        self.start(self.far, chunk, self.place.core_partner(), 6)
-
-    def rest(self, owners, chunk):
-        for owner in owners:
-            self.wait(owner + 1 - 2 * (owner % 2), chunk)
+        self.copy(self.pair, chunk, self.place.core_partner(), 0).wait_recv()
+        self.copy(self.pair, chunk, self.place.core_partner(), 3).start()
+        self.across(self.pair, chunk, self.place.other_chip(), 4, False)
+
+    def wait_across(self, owner, chunk):
+        amount = self.others.at[0, pl.ds(0, 256), :]
+        self.move(amount, amount, self.recv.at[4 + owner, chunk], self.place.core_partner(), 0).wait_recv()
+
+    def arrive_across(self, chunk):
+        for owner, lane in ((self.other, 5), (self.far, 6)):
+            self.wait_across(owner, chunk)
+            self.across(owner, chunk, self.place.core_partner(), lane, True)
+
+    def rest(self, chunk):
+        for owner in (self.mine, self.pair):
+            twin = owner + 1 - 2 * (owner % 2)
+            self.copy(twin, chunk, self.place.core_partner(), 0).wait_recv()
+
+    def rest_across(self, chunk):
+        for owner in (self.other, self.far):
+            self.wait_across(owner + 1 - 2 * (owner % 2), chunk)
 
     def finish(self):
         for lane in range(7):
-            sent(self.whole.at[pl.ds(0, 128), :], self.send.at[lane], self.place)
+            amount = self.whole.at[pl.ds(0, 128), :] if lane in (0, 1, 3) else self.others.at[:, pl.ds(0, 128), :]
+            sent(amount, self.send.at[lane], self.place)
 
 
 ROWS_SEMS = [pltpu.SemaphoreType.DMA((7,)), pltpu.SemaphoreType.DMA((8, CHUNKS))]
@@ -252,7 +259,8 @@
         self.place, self.part, self.land, self.send, self.recv = place, part, land, send, recv
 
     def own(self, kind, along, across, half):
-        return self.part.at[self.place.index(kind, along, across, half), pl.ds(kind * 128, 128), :]
+        block = self.place.index(kind, along, across, 0) // 2
+        return self.part.at[block, pl.ds((half * 2 + kind) * 128, 128), :]
 
     def copy(self, kind, block, spot, device):
         return pltpu.make_async_remote_copy(
@@ -297,8 +305,8 @@
 
         lax.fori_loop(0, 2, step, 0)
 
-    def first(self, kind):
-        for across in (2, 1, 3, 0):
+    def first(self, kind, offsets):
+        for across in offsets:
             for half, along in ((0, 1), (1, -1)):
                 block = self.own(kind, 2, across, half)
                 self.start(kind, block, half * 4 + across, self.place.device(kind, along, 0))
@@ -339,12 +347,9 @@
             self.start(kind, block, 26 + side * 2 + side, self.place.device(kind, 0, along))
 
     def fifth(self, kind, grad):
-        for half in (1 - self.place.h, self.place.h):
+        for half in range(2):
             self.wait_last(kind, half)
-        block = self.own(kind, 0, 0, 1 - self.place.h)
-        block[...] = self.summed(kind, 1 - self.place.h).astype(jnp.bfloat16)
-        self.start(kind, block, 30, self.place.partner())
-        grad[self.place.h, :, kind * 128 : (kind + 1) * 128] = self.summed(kind, self.place.h).T
+            grad[kind, :, half * 128 : (half + 1) * 128] = self.summed(kind, half).T
 
     def wait_last(self, kind, half):
         amount = self.land.at[kind, pl.ds(0, 2)]
@@ -363,11 +368,6 @@
             total = total + self.land[kind, 26 + side * 2 + half].astype(jnp.float32)
         return total
 
-    def last(self, kind, grad):
-        self.wait(kind, [30])
-        block = self.land[kind, 30].astype(jnp.float32)
-        grad[1 - self.place.h, :, kind * 128 : (kind + 1) * 128] = block.T
-
     def finish(self):
         for kind in range(2):
             sent(self.land.at[kind], self.send.at[kind], self.place)
@@ -389,7 +389,7 @@
 
 def turn(field, cosine, sine):
     parts = []
-    for head in range(2):
+    for head in range(field.shape[1] // HEAD):
         one = field[:, head * HEAD : (head + 1) * HEAD]
         parts.append(one * cosine + pltpu.roll(one, HEAD // 2, 1) * sine)
     return jnp.concatenate(parts, axis=1)
@@ -409,17 +409,21 @@
     return pl.ds(pl.multiple_of(head * HEAD, HEAD), HEAD)
 
 
-def base_head(head, query, cotangent, keys, values, key_sum, value_sum):
+def base_heads(head, count, query, cotangent, keys, values, key_sum, value_sum):
     group = head // 8
     for block in range(2):
-        rows, count = pl.ds(block * 256, 256), (block + 1) * 256
-        queries, pulls = query[rows, columns(head)], cotangent[rows, columns(head)]
-        weights = softmax_down(keys[:count, columns(group)], queries)
-        pulled = product_rows(values[:count, columns(group)], pulls)
-        mean = jnp.sum(weights * pulled, axis=0, keepdims=True)
-        back = (weights * (pulled - mean) * FACTOR).astype(BF16)
-        value_sum[:count, columns(group)] += product(weights.astype(BF16), pulls)
-        key_sum[:count, columns(group)] += product(back, queries)
+        rows, upto = pl.ds(block * 256, 256), (block + 1) * 256
+        key_part, value_part = 0.0, 0.0
+        for at in range(count):
+            queries, pulls = query[rows, columns(head + at)], cotangent[rows, columns(head + at)]
+            weights = softmax_down(keys[:upto, columns(group)], queries)
+            pulled = product_rows(values[:upto, columns(group)], pulls)
+            mean = jnp.sum(weights * pulled, axis=0, keepdims=True)
+            back = (weights * (pulled - mean) * FACTOR).astype(BF16)
+            value_part = value_part + product(weights.astype(BF16), pulls)
+            key_part = key_part + product(back, queries)
+        value_sum[:upto, columns(group)] += value_part
+        key_sum[:upto, columns(group)] += key_part
 
 
 def tangent_head(head, query, tangent, keys, key_tangent, turned, context, context_tangent):
@@ -439,13 +443,13 @@
         context_tangent[rows, columns(head)] = (first[HEAD:] + second).T.astype(BF16)
 
 
-def project(normed, start, weights, total, first, last):
+def project(normed, weights, total, first, last):
     def step(at, carry):
         for kind, weight in enumerate(weights):
             sums = 0.0
             for part in range(4):
                 index = at * 4 + part
-                left = normed[pl.ds(start, 512), pl.ds(pl.multiple_of(index * 256, 256), 256)]
+                left = normed[:, pl.ds(pl.multiple_of(index * 256, 256), 256)]
                 sums = sums + product(left, weight[index])
             total[:, kind * 256 : (kind + 1) * 256] += sums
         return carry
@@ -453,11 +457,25 @@
     lax.fori_loop(first, last, step, 0)
 
 
+def project_half(left, weight, total):
+    total[...] = jnp.zeros_like(total)
+
+    def step(at, carry):
+        for kind in range(2):
+            sums = 0.0
+            for part in range(4):
+                sums = sums + product(left(at * 4 + part), weight[at * 4 + part, kind])
+            total[:, kind * 256 : (kind + 1) * 256] += sums
+        return carry
+
+    lax.fori_loop(0, 4, step, 0)
+
+
 def layer_kernel(
     tokens, gain, query_in, tangent_in, kv_in, bias, task_in, bias_task, cotangent_in, cosine, sine,
     context_out, context_tangent_out, grad, bias_grad,
-    context, context_tangent, token_rows, query, tangent, cotangent, normed, base_all, task_own, task_all, part, land, total, task_total,
-    keys, values, kv_tangent, tangent_out, turned, key_sum, value_sum, back, back_kind, sums, sums_land,
+    context, context_tangent, token_rows, query, tangent, cotangent, normed, other_rows, base_all, task_all, part, land, total,
+    keys, values, kv_tangent, tangent_out, tangent_in_land, turned, key_sum, value_sum, back, back_other, sums, sums_land,
     local, out_sems, base_send, base_recv, task_send, task_recv, rows_send, rows_recv,
     part_send, part_recv, sums_send, sums_recv, pass_send, pass_recv,
 ):
@@ -470,8 +488,7 @@
         return copy
 
     waits = [load(kv_in.at[kind], base_all.at[kind, place.dp], kind) for kind in range(2)]
-    waits.append(load(task_in, task_own, 2))
-    waits.append(load(task_in.at[h], task_all.at[place.dp], 3))
+    waits.append(load(task_in, task_all.at[place.dp // 2], 2))
     load_tokens = load(tokens, token_rows, 4)
     later = [load(query_in, query, 5), load(cotangent_in, cotangent, 6), load(tangent_in, tangent, 7)]
     around = ring_devices(place) + [place.core_partner(), place.pair_chip(), place.other_chip()]
@@ -481,25 +498,21 @@
         return base_all.at[kind, index]
 
     def task_piece(kind, index):
-        return task_all.at[index, pl.ds(kind * 128, 128), :]
-
-    def task_partner(kind):
-        return task_own.at[1 - h, pl.ds(kind * 128, 128), :]
+        return task_all.at[index // 2, kind, pl.ds(pl.multiple_of(index % 2 * 128, 128), 128), :]
+
+    def task_sent(kind, count):
+        return task_all.at[pl.ds(0, count // 2), kind]
 
     base = Gather(
         place, base_piece, lambda kind: base_piece(kind, place.dp),
         lambda kind, count: base_all.at[kind, pl.ds(0, count)], base_send, base_recv,
     )
-    task = Gather(
-        place, task_piece, task_partner,
-        lambda kind, count: task_all.at[pl.ds(0, count), pl.ds(0, 128), :], task_send, task_recv,
-    )
-    rows = Rows(place, normed, rows_send, rows_recv)
+    task = Gather(place, task_piece, None, task_sent, task_send, task_recv)
+    rows = Rows(place, normed, other_rows, rows_send, rows_recv)
     for copy in waits:
         copy.wait()
     greeted(around)
     base.swap()
-    task.swap()
     base.first()
     load_tokens.wait()
     scale = gain[...]
@@ -523,8 +536,6 @@
         if at in (16, 19, 22, 26, 31):
             chunk = (16, 19, 22, 26, 31).index(at)
             rows.arrive_pair(chunk)
-            if chunk > 0:
-                rows.arrive_other(chunk - 1)
     task.first()
     ahead = [event for _, _, event in task.events()]
 
@@ -533,46 +544,24 @@
             ahead.pop(0)()
 
     events(2)
-    mine, others = pl.multiple_of(h * 512, 512), pl.multiple_of(512 - h * 512, 512)
     total[...] = jnp.zeros_like(total)
     both = [base_all.at[0], base_all.at[1]]
     rows.arrive_pair(5)
     for chunk in range(4):
-        rows.rest([rows.mine, rows.pair], chunk)
-    project(normed, mine, both, total, 0, 4)
+        rows.rest(chunk)
+    project(normed, both, total, 0, 4)
     for chunk in (4, 5, 6, 7):
         if chunk >= 6:
             rows.arrive_pair(chunk)
-        if chunk == 7:
-            for other in range(CHUNKS // 2):
-                rows.relay(other)
-            for other in range(4, 7):
-                rows.arrive_other(other)
-                rows.relay(other)
-        rows.rest([rows.mine, rows.pair], chunk)
-        project(normed, mine, both, total, chunk, chunk + 1)
-    rows.arrive_other(7)
-    rows.relay(7)
+        events((0, 0, 8, 4)[chunk - 4])
+        rows.rest(chunk)
+        project(normed, both, total, chunk, chunk + 1)
     keys[...] = turn(total[:, :256] + bias[0:1, :], cosine[...], sine[...]).astype(BF16)
     values[...] = (total[:, 256:] + bias[1:2, :]).astype(BF16)
-    events(8)
     key_sum[...] = jnp.zeros_like(key_sum)
     value_sum[...] = jnp.zeros_like(value_sum)
-    for part_of in range(8):
-
-        def base_step(at, carry, part_of=part_of):
-            base_head(part_of * 2 + at, query, cotangent, keys, values, key_sum, value_sum)
-            return carry
-
-        lax.fori_loop(0, 2, base_step, 0, unroll=2)
-        events((4, 0, 2, 4, 2, 4, 4, 4)[part_of])
-        for chunk in ((), (), (), (), (), (0, 4), (), (1, 5))[part_of]:
-            rows.arrive_far(chunk)
-
-    key_back = turn(key_sum[...], cosine[...], -sine[...]).astype(BF16)
-    value_back = value_sum[...].astype(BF16)
-    back[0] = key_back.astype(F32).T.astype(BF16)
-    back[1] = value_back.astype(F32).T.astype(BF16)
+    sums[0] = jnp.zeros_like(sums[0])
+    back_swaps = []
 
     def swap(source, target, at):
         return pltpu.make_async_remote_copy(
@@ -584,12 +573,23 @@
             device_id_type=MESH,
         )
 
-    back_swap = swap(back.at[1 - h], back_kind.at[h], 0)
-    back_swap.start()
-    back_kind[h] = back[h]
-    sums[0] = jnp.zeros_like(sums[0])
-    sums[0, 0:1, :] = jnp.sum(key_back.astype(F32), axis=0, keepdims=True)
-    sums[0, 1:2, :] = jnp.sum(value_back.astype(F32), axis=0, keepdims=True)
+    for part_of in range(4):
+        base_heads(part_of * 4, 4, query, cotangent, keys, values, key_sum, value_sum)
+        events((2, 6, 10, 4)[part_of])
+        for chunk in (part_of * 2, part_of * 2 + 1):
+            rows.arrive_across(chunk)
+        if part_of % 2 == 1:
+            group = part_of // 2
+            pick = slice(group * HEAD, (group + 1) * HEAD)
+            key_back = turn(key_sum[:, pick], cosine[...], -sine[...]).astype(BF16).astype(F32)
+            value_back = value_sum[:, pick].astype(BF16).astype(F32)
+            back[group * 256 : group * 256 + 128, :] = key_back.T.astype(BF16)
+            back[group * 256 + 128 : (group + 1) * 256, :] = value_back.T.astype(BF16)
+            here = pl.ds(group * 256, 256)
+            back_swaps.append(swap(back.at[here, :], back_other.at[here, :], group))
+            back_swaps[-1].start()
+            sums[0, 0:1, pick] = jnp.sum(key_back, axis=0, keepdims=True)
+            sums[0, 1:2, pick] = jnp.sum(value_back, axis=0, keepdims=True)
 
     odd_y, odd_z = place.y % 2, place.z % 2
     mates = [
@@ -619,58 +619,43 @@
     mate_copy(0).start()
     events(len(ahead))
 
-    is_key = (h == 0).astype(F32)
-    kind_cosine = cosine[...] * is_key + (1.0 - is_key)
-    kind_sine = sine[...] * is_key
-    kind_bias = jnp.where(h == 0, bias_task[0:1, :], bias_task[1:2, :])
-    task_total[...] = jnp.zeros_like(task_total)
-    project(normed, mine, [task_all], task_total, 0, 8)
-    kv_tangent[h] = turn(task_total[...] + kind_bias, kind_cosine, kind_sine).astype(BF16)
-    task_total[...] = jnp.zeros_like(task_total)
-
-    def project_others(chunks):
-        for chunk in chunks:
-            rows.rest([rows.other, rows.far], chunk)
-            project(normed, others, [task_all], task_total, chunk, chunk + 1)
-
+    for chunk in range(CHUNKS):
+        rows.rest_across(chunk)
+    project_half(lambda block: other_rows[block], task_all, total)
+    tangent_out[...] = total[...].astype(BF16)
+    tangent_swaps = []
+    for kind in range(2):
+        pick = pl.ds(kind * 256, 256)
+        tangent_swaps.append(swap(tangent_out.at[:, pick], tangent_in_land.at[:, pick], 2 + kind))
+        tangent_swaps[-1].start()
     mate_sum(0)
-    for chunk in (2, 6):
-        rows.arrive_far(chunk)
-    project_others((0, 1, 4, 5))
-    mate_sum(1)
-    for chunk in (3, 7):
-        rows.arrive_far(chunk)
-    project_others((2, 6))
-    mate_sum(2)
-    for chunk in (3, 7):
-        rows.rest([rows.other, rows.far], chunk)
-    back_swap.wait_recv()
+
+    def half_columns(block):
+        return pl.ds(pl.multiple_of(block * 512 + h * 256, 256), 256)
+
+    project_half(lambda block: normed[:, half_columns(block)], task_all, total)
+    for copy in back_swaps:
+        copy.wait_recv()
 
     scatter = Scatter(place, part, land, part_send, part_recv)
 
     def gradients(count, offsets):
         def step(at, carry):
             off_y, off_z = offsets(at)
-            index = ((place.z + off_z) % 4) * 8 + ((place.y + off_y) % 4) * 2
-            pick = pl.ds(pl.multiple_of(index * 256, 512), 512)
-            block = product(back_kind[0], normed[:512, pick]) + product(back_kind[1], normed[512:, pick])
-            block = block.astype(BF16)
-            part[index] = block[:, :256]
-            part[index + 1] = block[:, 256:]
+            block = ((place.z + off_z) % 4) * 4 + (place.y + off_y) % 4
+            own = product(back[...], normed[:, half_columns(block)])
+            part[block] = (own + product(back_other[...], other_rows[block])).astype(BF16)
             return carry
 
         lax.fori_loop(0, count, step, 0)
 
-    gradients(4, lambda at: (2, at))
-    scatter.first(0)
+    gradients(2, lambda at: (2, 2 + at))
+    scatter.first(0, (2, 3))
+    gradients(2, lambda at: (2, at))
+    scatter.first(0, (1, 0))
     gradients(3, lambda at: (3 + at, 2))
-    scatter.first(1)
-    mate_sum(3)
-    for chunk in (3, 7):
-        project(normed, others, [task_all], task_total, chunk, chunk + 1)
-    tangent_out[...] = turn(task_total[...] + kind_bias, kind_cosine, kind_sine).astype(BF16)
-    tangent_swap = swap(tangent_out, kv_tangent.at[h], 1)
-    tangent_swap.start()
+    scatter.first(1, (2, 3, 1, 0))
+    mate_sum(1)
     gradients(6, lambda at: (1 + 2 * (at // 3), 3 + at % 3))
     gradients(3, lambda at: (0, 3 + at))
 
@@ -687,44 +672,62 @@
             outs.append(pltpu.make_async_copy(source.at[:, pick], target.at[:, pick], out_sems.at[len(outs)]))
             outs[-1].start()
 
-    for across in (2, 1, 3, 0):
+    def second(across):
         for kind in range(2):
             scatter.second_own(kind, across)
         for kind in range(2):
             scatter.second(kind, across)
-    tangent_swap.wait_recv()
-    for group in range(2):
-        pick = slice(group * HEAD, (group + 1) * HEAD)
-        turned[group, :HEAD, :] = values[:, pick].astype(F32).T.astype(BF16)
-        turned[group, HEAD:, :] = kv_tangent[1, :, pick].astype(F32).T.astype(BF16)
+
+    second(2)
+    second(3)
+    second(1)
+    mate_sum(2)
+    def turn_values():
+        for copy in tangent_swaps:
+            copy.wait_recv()
+        key = total[:, :256] + tangent_in_land[:, :256].astype(F32) + bias_task[0:1, :]
+        kv_tangent[0] = turn(key, cosine[...], sine[...]).astype(BF16)
+        value = total[:, 256:] + tangent_in_land[:, 256:].astype(F32) + bias_task[1:2, :]
+        kv_tangent[1] = value.astype(BF16)
+        for group in range(2):
+            pick = slice(group * HEAD, (group + 1) * HEAD)
+            turned[group, :HEAD, :] = values[:, pick].astype(F32).T.astype(BF16)
+            turned[group, HEAD:, :] = kv_tangent[1, :, pick].astype(F32).T.astype(BF16)
+
     def third(across):
         for kind in range(2):
             scatter.third(kind, across)
 
-    tangents(0, 4)
+    def third(across):
+        for kind in range(2):
+            scatter.third(kind, across)
+
+    turn_values()
+    tangents(0, 2)
     third(2)
-    tangents(4, 4)
+    second(0)
+    tangents(2, 4)
+    third(3)
     third(1)
-    third(3)
-    tangents(8, 4)
+    mate_sum(3)
     for kind in range(2):
         scatter.fourth(kind)
+    tangents(6, 4)
     third(0)
+    tangents(10, 2)
     for kind in range(2):
         scatter.fifth(kind, grad)
-    tangents(12, 4)
     mate_sum(4)
     bias_grad[...] = sums[5, 0:2, :]
-    for kind in range(2):
-        scatter.last(kind, grad)
+    tangents(12, 4)
     for copy in outs:
         copy.wait()
     scatter.finish()
     base.finish()
     task.finish()
     rows.finish()
-    back_swap.wait_send()
-    tangent_swap.wait_send()
+    for copy in back_swaps + tangent_swaps:
+        copy.wait_send()
 
 
 def layer(*operands):
@@ -737,27 +740,27 @@
         pltpu.VMEM((512, 2048), BF16),
         pltpu.VMEM((512, 2048), BF16),
         pltpu.VMEM((512, 2048), BF16),
-        pltpu.VMEM((1024, 8192), BF16),
+        pltpu.VMEM((512, 8192), BF16),
+        pltpu.VMEM((16, 512, 256), BF16),
         pltpu.VMEM((2, 32, 256, 256), BF16),
-        pltpu.VMEM((2, 256, 256), BF16),
-        pltpu.VMEM((32, 256, 256), BF16),
-        pltpu.VMEM((32, 256, 256), BF16),
-        pltpu.VMEM((2, 31, 128, 256), BF16),
+        pltpu.VMEM((16, 2, 256, 256), BF16),
+        pltpu.VMEM((16, 512, 256), BF16),
+        pltpu.VMEM((2, 30, 128, 256), BF16),
         pltpu.VMEM((512, 512), F32),
-        pltpu.VMEM((512, 256), F32),
         pltpu.VMEM((512, 256), BF16),
         pltpu.VMEM((512, 256), BF16),
         pltpu.VMEM((2, 512, 256), BF16),
-        pltpu.VMEM((512, 256), BF16),
+        pltpu.VMEM((512, 512), BF16),
+        pltpu.VMEM((512, 512), BF16),
         pltpu.VMEM((2, 256, 512), BF16),
         pltpu.VMEM((512, 256), F32),
         pltpu.VMEM((512, 256), F32),
-        pltpu.VMEM((2, 256, 512), BF16),
-        pltpu.VMEM((2, 256, 512), BF16),
+        pltpu.VMEM((512, 512), BF16),
+        pltpu.VMEM((512, 512), BF16),
         pltpu.VMEM((6, 8, 256), F32),
         pltpu.VMEM((5, 8, 256), F32),
         pltpu.SemaphoreType.DMA((8,)),
-        pltpu.SemaphoreType.DMA((8,)),
+        pltpu.SemaphoreType.DMA((14,)),
         *GATHER_SEMS,
         *GATHER_SEMS,
         *ROWS_SEMS,
@@ -765,8 +768,8 @@
         pltpu.SemaphoreType.DMA((2, 31)),
         pltpu.SemaphoreType.DMA((5,)),
         pltpu.SemaphoreType.DMA((5,)),
-        pltpu.SemaphoreType.DMA((2,)),
-        pltpu.SemaphoreType.DMA((2,)),
+        pltpu.SemaphoreType.DMA((4,)),
+        pltpu.SemaphoreType.DMA((4,)),
     ]
     return pl.pallas_call(
         layer_kernel,

time: 135 us -> 128 us (0.948)
  Pallas kernels: 134 us -> 127 us
    pallas_call x1, Pallas kernels: 130 us -> 123 us  [layer(): pl.pallas_call(layer_kernel, out_shape=(jax.ShapeDtypeStruct((512, 2048),...]
where the time goes in v5:
time: 128 us
  Pallas kernels  127 us (99%)
    pallas_call x1, Pallas kernels, layer(): pl.pallas_call(layer_kernel, out_shape=(jax.ShapeDtypeStruct((512, 2048),...  123 us
    pallas_call x1, Pallas kernels, hand_over(): pl.pallas_call(hand_over_kernel, out_shape=tuple((jax.ShapeDtypeStruct(on...  4.18 us

profile of v5, /device:TPU:0, one launch (start us, length us, event | category | flops | bytes accessed | tf_op | source)
XLA Modules:
  0.0 128.0 jit_solution(14922084466941263098)
XLA Ops:
  0.6 123.0 %layer.1 = (bf16[512,2048]{1,0:T(8,128)(2,1)}, bf16[512,2048]{1,0:T(8,128)(2,1)}, f32[2,256,256]{2,1,0:T(8,128)}, f32[2,256]{1,0:T(2,128)}) custom-call(bf16[128,8192]{1,0:T(8,128)(2,1)} %tokens.1, f32[1,8192]{1,0:T(1,128)} %bitcast.1, bf16[512,2048]{1,0:T(8,128)(2,1)} %query_in.1, bf16[512,2048]{1,0:T(8,128)(2,1)} %tangent_in.1, ...), custom_call_target="tpu_custom_call" | custom-call | tf_op jit(solution)/shard_map/layer/pallas_call | solution.py:774
  123.7 4.2 %hand_over.1 = (bf16[512,2048]{1,0:T(8,128)(2,1)}, bf16[512,2048]{1,0:T(8,128)(2,1)}, f32[2,256,256]{2,1,0:T(8,128)}, f32[2,256]{1,0:T(2,128)}) custom-call(bf16[512,2048]{1,0:T(8,128)(2,1)} %get-tuple-element.8.context, bf16[512,2048]{1,0:T(8,128)(2,1)} %get-tuple-element.9.context_tangent, f32[2,256,256]{2,1,0:T(8,128)} %get-tuple-element.10.grad, ...), custom_call_target="tpu_custom_call" | custom-call | tf_op jit(solution)/shard_map/hand_over/pallas_call | solution.py:814

commit v6 on v5

--- a/solution.py
+++ b/solution.py
@@ -715,11 +715,11 @@
     tangents(6, 4)
     third(0)
     tangents(10, 2)
+    tangents(12, 4)
     for kind in range(2):
         scatter.fifth(kind, grad)
     mate_sum(4)
     bias_grad[...] = sums[5, 0:2, :]
-    tangents(12, 4)
     for copy in outs:
         copy.wait()
     scatter.finish()

time: 128 us -> 127 us (level)
  no operation moved by 1% of the time
where the time goes in v6:
time: 127 us
  Pallas kernels  126 us (99%)
    pallas_call x1, Pallas kernels, layer(): pl.pallas_call(layer_kernel, out_shape=(jax.ShapeDtypeStruct((512, 2048),...  122 us
    pallas_call x1, Pallas kernels, hand_over(): pl.pallas_call(hand_over_kernel, out_shape=tuple((jax.ShapeDtypeStruct(on...  4.18 us

profile of v6, /device:TPU:0, one launch (start us, length us, event | category | flops | bytes accessed | tf_op | source)
XLA Modules:
  0.0 127.3 jit_solution(6792021319671684239)
XLA Ops:
  0.6 122.3 %layer.1 = (bf16[512,2048]{1,0:T(8,128)(2,1)}, bf16[512,2048]{1,0:T(8,128)(2,1)}, f32[2,256,256]{2,1,0:T(8,128)}, f32[2,256]{1,0:T(2,128)}) custom-call(bf16[128,8192]{1,0:T(8,128)(2,1)} %tokens.1, f32[1,8192]{1,0:T(1,128)} %bitcast.1, bf16[512,2048]{1,0:T(8,128)(2,1)} %query_in.1, bf16[512,2048]{1,0:T(8,128)(2,1)} %tangent_in.1, ...), custom_call_target="tpu_custom_call" | custom-call | tf_op jit(solution)/shard_map/layer/pallas_call | solution.py:774
  122.9 4.2 %hand_over.1 = (bf16[512,2048]{1,0:T(8,128)(2,1)}, bf16[512,2048]{1,0:T(8,128)(2,1)}, f32[2,256,256]{2,1,0:T(8,128)}, f32[2,256]{1,0:T(2,128)}) custom-call(bf16[512,2048]{1,0:T(8,128)(2,1)} %get-tuple-element.8.context, bf16[512,2048]{1,0:T(8,128)(2,1)} %get-tuple-element.9.context_tangent, f32[2,256,256]{2,1,0:T(8,128)} %get-tuple-element.10.grad, ...), custom_call_target="tpu_custom_call" | custom-call | tf_op jit(solution)/shard_map/hand_over/pallas_call | solution.py:814
